TPU v7x, 32 devices: a whole 2x2x4 slice. The times are simulated.
32 devices in a mesh: leaf: 8 (over z, x), col: 4 (over y, core).
Axes of the slice: x: 2, y: 2, z: 4, core: 2. Of those that a mesh axis runs over, the one named last changes fastest.
Arguments:
- right_side: bfloat16 [16384, 256], P('leaf'), may hold values from -6 to 6
- x_blocks: bfloat16 [8, 4, 96, 128, 128], P('leaf', 'col'), may hold values from -0.109375 to 0.109375
- row_ids: int32 [8, 4, 96], P('leaf', 'col'), may hold values from 0 to 15
- col_ids: int32 [8, 4, 96], P('leaf', 'col'), may hold values from 0 to 7
- counts: int32 [8, 4], P('leaf', 'col'), may hold values from 48 to 96, as said below
Outputs:
- solution: bfloat16 [16384, 256], P(('leaf', 'col'))
Inputs may be any that keep to these rules, and one draw needn't show every extreme that they name: `row_ids`: block rows index the rows of the device's own subtree. `col_ids`: slots below 2 are the subtree's own columns; slot 2 + (l - 1) * 2 + s is column s of the level-l separator. `counts`: some device uses all 96 slots; slots past a device's count are unused.
All inputs are finite; a program needn't handle non-finite values.
Results may differ from a plain program's by a relative error of at most 0.0047.
Values may be sent and summed in bfloat16 or wider, within the bound.
No kernel may reach another device: no remote copies, remote signals or barrier semaphores. Data moves between devices by JAX's collectives and lax.ppermute only.
A program may use at most 128 MiB of HBM per device.

v0:
```python
import jax
import jax.numpy as jnp
from jax import lax
from jax.sharding import PartitionSpec as P

CI = 2
SEP = 2


def from_partner(x, axis, apart):
    return lax.ppermute(x, axis, [(i, i ^ 1 << apart) for i in range(lax.axis_size(axis))])


def body(right_side, x_blocks, row_ids, col_ids, counts):
    blocks = x_blocks[0, 0]
    block_rows = row_ids[0, 0]
    block_cols = col_ids[0, 0]
    live_count = counts[0, 0]
    list_len = blocks.shape[0]
    block_size = blocks.shape[1]
    columns = right_side.shape[1]
    row_blocks = right_side.shape[0] // block_size
    levels = lax.axis_size("leaf").bit_length() - 1
    slot_total = CI + levels * SEP
    alive_weight = (lax.iota(jnp.int32, list_len) < live_count).astype(jnp.float32)[:, None, None]
    rhs_blocks = right_side.reshape(row_blocks, block_size, columns)
    picked = rhs_blocks[block_rows]
    products = jnp.einsum("kab,kac->kbc", blocks, picked, preferred_element_type=jnp.float32)
    partial_value = (
        jnp.zeros((slot_total, block_size, columns), jnp.float32)
        .at[block_cols]
        .add(products * alive_weight)
    )
    interior = partial_value[:CI]
    separators = partial_value[CI:].reshape(levels, SEP, block_size, columns)
    for level_bit in range(levels):
        pending = separators[level_bit:]
        incoming = from_partner(pending, "leaf", level_bit)
        separators = jnp.concatenate([separators[:level_bit], pending + incoming], axis=0)
    finished_seps = separators.reshape(levels * SEP, block_size, columns)
    coarse = jnp.concatenate([interior, finished_seps], axis=0).astype(jnp.bfloat16)
    gathered = coarse[block_cols]
    image = jnp.einsum("kab,kbc->kac", blocks, gathered, preferred_element_type=jnp.float32)
    terms = (
        jnp.zeros((row_blocks, block_size, columns), jnp.float32)
        .at[block_rows]
        .add(image * alive_weight)
    )
    terms = terms.reshape(row_blocks * block_size, columns)
    return lax.psum_scatter(terms, "col", scatter_dimension=0, tiled=True).astype(jnp.bfloat16)


def solution(mesh):
    in_specs = (
        P("leaf", None),
        P("leaf", "col", None, None, None),
        P("leaf", "col", None),
        P("leaf", "col", None),
        P("leaf", "col"),
    )
    out_specs = P(("leaf", "col"), None)
    return jax.shard_map(body, mesh=mesh, in_specs=in_specs, out_specs=out_specs, check_vma=False)
```

profile of v0, /device:TPU:0, one launch (start us, length us, event | category | flops | bytes accessed | tf_op | source)
XLA Modules:
  0.0 216.3 jit_solution(6181259875130613597)
XLA Ops:
  6.5 0.0 copy-start
  6.5 0.0 reduce-scatter.2.cloned.1.call-start
  6.5 0.8 fusion.5
  8.2 7.2 %gather_fusion = bf16[96,128,256]{2,1,0:T(8,128)(2,1)} fusion(bf16[16,128,256]{2,1,0:T(8,128)(2,1)} %bitcast.26, s32[1024]{0:T(1024)S(1)} %pad_clamp_fusion.1), kind=kCustom, calls=%fused_computation | custom fusion | bytes 12583296 | tf_op jit(solution)/shard_map/gather | solution.py:27
  15.4 0.0 copy-done
  15.4 9.8 %multiply_bitcast_fusion.1 = f32[96,128,256]{1,2,0:T(8,128)} fusion(f32[96]{0:T(128)S(1)} %compare_convert_fusion, bf16[96,128,256]{2,1,0:T(8,128)(2,1)} %gather_fusion, bf16[1,1,96,128,128]{4,3,2,1,0:T(8,128)(2,1)S(1)} %copy-done), kind=kOutput, calls=%fused_computation.5 | convolution fusion | flops 808452096 | bytes 22020480 | tf_op jit(solution)/shard_map/kab,kac->kbc/dot_general | solution.py:28
  25.2 0.0 copy-start.2
  25.2 12.6 %copy.9 = f32[96,128,256]{2,1,0:T(8,128)} copy(f32[96,128,256]{1,2,0:T(8,128)} %multiply_bitcast_fusion.1) | data formatting | bytes 25165824 | tf_op jit(solution)/shard_map/mul | solution.py:32
  37.8 0.0 copy-done.2
  37.8 1.1 broadcast_in_dim.5
  38.9 27.7 %scatter_fusion = f32[8,128,256]{2,1,0:T(8,128)} fusion(f32[8,128,256]{2,1,0:T(8,128)} %broadcast_in_dim.5, s32[96]{0:T(128)S(1)} %fusion.6, f32[96,128,256]{2,1,0:T(8,128)} %copy.9), kind=kCustom, calls=%fused_computation.2 | custom fusion | flops 3145728 | bytes 37749120 | tf_op jit(solution)/shard_map/scatter-add | solution.py:32
  66.6 1.2 slice.32
  67.8 2.9 %collective-permute-start = (f32[3,2,128,256]{3,2,1,0:T(8,128)S(1)}, f32[3,2,128,256]{3,2,1,0:T(8,128)S(1)}, u32[]{:S(2)}, u32[]{:S(2)}) collective-permute-start(f32[3,2,128,256]{3,2,1,0:T(8,128)S(1)} %bitcast.27), channel_id=1, source_target_pairs={{0,4},{4,0},{8,12},{12,8},{16,20},{20,16},{24,28},{28,24},{1,5},{5... | collective-permute-start | bytes 2359304 | tf_op jit(solution)/shard_map/ppermute | solution.py:11
  70.6 17.6 %collective-permute-done = f32[3,2,128,256]{3,2,1,0:T(8,128)S(1)} collective-permute-done((f32[3,2,128,256]{3,2,1,0:T(8,128)S(1)}, f32[3,2,128,256]{3,2,1,0:T(8,128)S(1)}, u32[]{:S(2)}, u32[]{:S(2)}) %collective-permute-start) | collective-permute-done | bytes 786464 | tf_op jit(solution)/shard_map/ppermute | solution.py:11
  88.3 0.1 add.39
  88.4 1.8 collective-permute-start.1
  90.2 11.4 %collective-permute-done.1 = f32[2,2,128,256]{3,2,1,0:T(8,128)S(1)} collective-permute-done((f32[2,2,128,256]{3,2,1,0:T(8,128)S(1)}, f32[2,2,128,256]{3,2,1,0:T(8,128)S(1)}, u32[]{:S(2)}, u32[]{:S(2)}) %collective-permute-start.1) | collective-permute-done | bytes 524320 | tf_op jit(solution)/shard_map/ppermute | solution.py:11
  101.7 0.1 fusion.7
  101.8 2.6 %collective-permute-start.2 = (f32[1,2,128,256]{3,2,1,0:T(8,128)S(1)}, f32[1,2,128,256]{3,2,1,0:T(8,128)S(1)}, u32[]{:S(2)}, u32[]{:S(2)}) collective-permute-start(f32[1,2,128,256]{3,2,1,0:T(8,128)S(1)} %slice.35), channel_id=1, source_target_pairs={{0,16},{4,20},{8,24},{12,28},{16,0},{20,4},{24,8},{28,12},{1,17},{... | collective-permute-start | bytes 786440 | tf_op jit(solution)/shard_map/ppermute | solution.py:11
  104.4 1.0 slice.41
  105.4 9.7 %collective-permute-done.2 = f32[1,2,128,256]{3,2,1,0:T(8,128)S(1)} collective-permute-done((f32[1,2,128,256]{3,2,1,0:T(8,128)S(1)}, f32[1,2,128,256]{3,2,1,0:T(8,128)S(1)}, u32[]{:S(2)}, u32[]{:S(2)}) %collective-permute-start.2) | collective-permute-done | bytes 262176 | tf_op jit(solution)/shard_map/ppermute | solution.py:11
  115.1 0.8 pad_maximum_fusion
  116.0 7.0 %gather_fusion.1 = bf16[96,128,256]{2,1,0:T(8,128)(2,1)} fusion(bf16[8,128,256]{2,1,0:T(8,128)(2,1)} %pad_maximum_fusion, s32[1024]{0:T(1024)S(1)} %pad_clamp_fusion), kind=kCustom, calls=%fused_computation.1 | custom fusion | bytes 12583296 | tf_op jit(solution)/shard_map/gather | solution.py:42
  123.0 9.8 %multiply_bitcast_fusion = f32[96,128,256]{1,2,0:T(8,128)} fusion(f32[96]{0:T(128)S(1)} %compare_convert_fusion, bf16[96,128,256]{2,1,0:T(8,128)(2,1)} %gather_fusion.1, bf16[1,1,96,128,128]{4,3,2,1,0:T(8,128)(2,1)S(1)} %copy-done), kind=kOutput, calls=%fused_computation.4 | convolution fusion | flops 808452096 | bytes 22020480 | tf_op jit(solution)/shard_map/kab,kbc->kac/dot_general | solution.py:43
  132.8 12.6 %copy.11 = f32[96,128,256]{2,1,0:T(8,128)} copy(f32[96,128,256]{1,2,0:T(8,128)} %multiply_bitcast_fusion) | data formatting | bytes 25165824 | tf_op jit(solution)/shard_map/mul | solution.py:47
  145.4 1.6 broadcast_in_dim.4
  146.9 0.0 copy-start.1
  146.9 28.3 %scatter_fusion.1 = f32[16,128,256]{2,1,0:T(8,128)} fusion(f32[16,128,256]{2,1,0:T(8,128)} %broadcast_in_dim.4, s32[96]{0:T(128)S(1)} %fusion.5, f32[96,128,256]{2,1,0:T(8,128)} %copy.11), kind=kCustom, calls=%fused_computation.3 | custom fusion | flops 3145728 | bytes 37749120 | tf_op jit(solution)/shard_map/scatter-add | solution.py:47
  175.3 0.0 reduce-scatter.2.cloned.1.call-update
  175.3 32.4 %reduce-scatter.2.cloned.1.call-done = f32[512,256]{1,0:T(8,128)} async-done(((f32[2048,256]{1,0:T(8,128)}), f32[512,256]{1,0:T(8,128)}) %reduce-scatter.2.cloned.1.call-update) | async-done | bytes 524304 | tf_op jit(solution)/shard_map/reduce_scatter | solution.py:50
  207.7 1.8 convert_element_type.12
  209.5 0.0 copy-done.1
  (9 shorter events, 0.2 us)
Async XLA Ops:
  6.5 8.8 %copy-start = (bf16[1,1,96,128,128]{4,3,2,1,0:T(8,128)(2,1)S(1)}, bf16[1,1,96,128,128]{4,3,2,1,0:T(8,128)(2,1)}, u32[]{:S(2)}) copy-start(bf16[1,1,96,128,128]{4,3,2,1,0:T(8,128)(2,1)} %param.6) | copy-start | bytes 9437188
  6.5 201.1 %reduce-scatter.2.cloned.1.call-start = ((), (), s32[]{:S(2)}) async-start(), calls=%async_computation.1 | async-start | bytes 2621440 | tf_op jit(solution)/shard_map/reduce_scatter | solution.py:50
  25.2 12.6 %copy-start.2 = (s32[1,1,96]{2,1,0:T(1,128)S(1)}, s32[1,1,96]{2,1,0:T(1,128)}, u32[]{:S(2)}) copy-start(s32[1,1,96]{2,1,0:T(1,128)} %param.8) | copy-start | bytes 1156
  67.8 20.5 %collective-permute-start = (f32[3,2,128,256]{3,2,1,0:T(8,128)S(1)}, f32[3,2,128,256]{3,2,1,0:T(8,128)S(1)}, u32[]{:S(2)}, u32[]{:S(2)}) collective-permute-start(f32[3,2,128,256]{3,2,1,0:T(8,128)S(1)} %bitcast.27), channel_id=1, source_target_pairs={{0,4},{4,0},{8,12},{12,8},{16,20},{20,16},{24,28},{28,24},{1,5},{5... | collective-permute-start | bytes 2359304 | tf_op jit(solution)/shard_map/ppermute | solution.py:11
  88.4 13.3 %collective-permute-start.1 = (f32[2,2,128,256]{3,2,1,0:T(8,128)S(1)}, f32[2,2,128,256]{3,2,1,0:T(8,128)S(1)}, u32[]{:S(2)}, u32[]{:S(2)}) collective-permute-start(f32[2,2,128,256]{3,2,1,0:T(8,128)S(1)} %slice.34), channel_id=1, source_target_pairs={{0,8},{4,12},{8,0},{12,4},{16,24},{20,28},{24,16},{28,20},{1,9},{5... | collective-permute-start | bytes 1572872 | tf_op jit(solution)/shard_map/ppermute | solution.py:11
  101.8 13.2 %collective-permute-start.2 = (f32[1,2,128,256]{3,2,1,0:T(8,128)S(1)}, f32[1,2,128,256]{3,2,1,0:T(8,128)S(1)}, u32[]{:S(2)}, u32[]{:S(2)}) collective-permute-start(f32[1,2,128,256]{3,2,1,0:T(8,128)S(1)} %slice.35), channel_id=1, source_target_pairs={{0,16},{4,20},{8,24},{12,28},{16,0},{20,4},{24,8},{28,12},{1,17},{... | collective-permute-start | bytes 786440 | tf_op jit(solution)/shard_map/ppermute | solution.py:11
  146.9 62.5 %copy-start.1 = (bf16[1,1,96,128,128]{4,3,2,1,0:T(8,128)(2,1)S(1)}, bf16[1,1,96,128,128]{4,3,2,1,0:T(8,128)(2,1)}, u32[]{:S(2)}) copy-start(bf16[1,1,96,128,128]{4,3,2,1,0:T(8,128)(2,1)} %param.6) | copy-start | bytes 9437188
Sparse Core Ops, SparseCore 0:
  175.4 32.2 reduce-scatter.1
where the time goes:
time: 217 us; the launch traced here: 216 us
  waiting for transfers between devices  71.1 us (33%)
  other arithmetic  59.7 us (28%)
  local copies, waits for them, and re-layouts  44.3 us (20%)
  matrix products  19.7 us (9%)
  between operations  14.3 us (7%)
  starting transfers between devices  7.25 us (3%)
    ppermute x3, waiting for transfers between devices, from_partner(): lax.ppermute(x, axis, [(i, i ^ 1 << apart) for i in range(lax.axis_size(a...  38.7 us
    reduce_scatter x1, waiting for transfers between devices, body(): lax.psum_scatter(terms, 'col', scatter_dimension=0, tiled=True)  32.4 us
    scatter-add x1, other arithmetic, body(): terms = jnp.zeros((row_blocks, block_size, columns), jnp.float32).at[bloc...  28.3 us
    scatter-add x1, other arithmetic, body(): partial_value = jnp.zeros((slot_total, block_size, columns), jnp.float32)...  27.7 us
    mul x1, local copies, waits for them, and re-layouts, body(): products * alive_weight  12.6 us
    mul x1, local copies, waits for them, and re-layouts, body(): image * alive_weight  12.6 us
    dot_general x1, matrix products, body(): jnp.einsum('kab,kbc->kac', blocks, gathered, preferred_element_type=jnp.f...  9.84 us
    dot_general x1, matrix products, body(): jnp.einsum('kab,kac->kbc', blocks, picked, preferred_element_type=jnp.flo...  9.84 us
  transfers between devices with their start and end apart: 4, of which 4 were waited for; matrix products, arithmetic and copies ran while one was open for 0% of the time, Pallas kernels for 0%

commit v1 on v0

v1 whole, which is shorter than its diff:
```python
import jax
import jax.numpy as jnp
from jax import lax
from jax.experimental import pallas as pl
from jax.experimental.pallas import tpu as pltpu
from jax.sharding import PartitionSpec as P

CI = 2
SEP = 2
UNROLL = 4
VMEM_LIMIT = 48 << 20


def swap(x, axis, bit):
    return lax.ppermute(x, axis, [(i, i ^ bit) for i in range(lax.axis_size(axis))])


def over_slots(count, list_len, one):
    def group(j, carry):
        for u in range(UNROLL):
            slot = j * UNROLL + u
            one(jnp.minimum(slot, list_len - 1), slot < count)
        return carry

    lax.fori_loop(0, (count + UNROLL - 1) // UNROLL, group, 0)


def gather_kernel(rhs_ref, x_ref, row_ref, col_ref, count_ref, part_ref, half_ref, acc_ref):
    list_len, block, _ = x_ref.shape
    slots = part_ref.shape[0]
    acc_ref[...] = jnp.zeros_like(acc_ref)

    def one(k, used):
        row = pl.multiple_of(row_ref[k] * block, block)
        col = jnp.where(used, col_ref[k], slots)
        acc_ref[col] += lax.dot_general(
            x_ref[k], rhs_ref[pl.ds(row, block), :], (((0,), (0,)), ((), ())), preferred_element_type=jnp.float32
        )

    over_slots(count_ref[0], list_len, one)
    for c in range(slots):
        part_ref[c] = acc_ref[c]
        half_ref[c] = acc_ref[c].astype(jnp.bfloat16)


def image_kernel(coarse_ref, x_ref, row_ref, col_ref, count_ref, side_ref, keep_ref, send_ref, acc_ref):
    list_len, block, _ = x_ref.shape
    groups, per = keep_ref.shape[:2]
    rows = 2 * groups * per
    acc_ref[...] = jnp.zeros_like(acc_ref)

    def one(k, used):
        row = jnp.where(used, row_ref[k], rows)
        acc_ref[row] += jnp.dot(x_ref[k], coarse_ref[col_ref[k]], preferred_element_type=jnp.float32)

    over_slots(count_ref[0], list_len, one)
    side = side_ref[0]
    for g in range(groups):
        for b in range(per):
            keep_ref[g, b] = acc_ref[(2 * g + side) * per + b]
            send_ref[g, b] = acc_ref[(2 * g + 1 - side) * per + b].astype(jnp.bfloat16)


def body(right_side, x_blocks, row_ids, col_ids, counts):
    blocks, block_rows, block_cols, count = x_blocks[0, 0], row_ids[0, 0], col_ids[0, 0], counts[0]
    block = blocks.shape[1]
    columns = right_side.shape[1]
    row_blocks = right_side.shape[0] // block
    levels = lax.axis_size("leaf").bit_length() - 1
    n_col = lax.axis_size("col")
    slots = CI + levels * SEP
    vmem = pl.BlockSpec(memory_space=pltpu.VMEM)
    smem = pl.BlockSpec(memory_space=pltpu.SMEM)
    params = pltpu.CompilerParams(vmem_limit_bytes=VMEM_LIMIT)

    part, half = pl.pallas_call(
        gather_kernel,
        out_shape=(
            jax.ShapeDtypeStruct((slots, block, columns), jnp.float32),
            jax.ShapeDtypeStruct((slots, block, columns), jnp.bfloat16),
        ),
        in_specs=[vmem, vmem, smem, smem, smem],
        out_specs=(vmem, vmem),
        scratch_shapes=[pltpu.VMEM((slots + 1, block, columns), jnp.float32)],
        compiler_params=params,
    )(right_side, blocks, block_rows, block_cols, count)

    done = [half[:CI]]
    own, sent = part[CI:], half[CI:]
    for level in range(levels):
        own = own + swap(sent, "leaf", 1 << level).astype(jnp.float32)
        both = own.astype(jnp.bfloat16)
        done.append(both[:SEP])
        own, sent = own[SEP:], both[SEP:]
    coarse = jnp.concatenate(done, axis=0)

    per = row_blocks // n_col
    side = (lax.axis_index("col") % 2).astype(jnp.int32)
    keep, send = pl.pallas_call(
        image_kernel,
        out_shape=(
            jax.ShapeDtypeStruct((n_col // 2, per, block, columns), jnp.float32),
            jax.ShapeDtypeStruct((n_col // 2, per, block, columns), jnp.bfloat16),
        ),
        in_specs=[vmem, vmem, smem, smem, smem, smem],
        out_specs=(vmem, vmem),
        scratch_shapes=[pltpu.VMEM((row_blocks + 1, block, columns), jnp.float32)],
        compiler_params=params,
    )(coarse, blocks, block_rows, block_cols, count, side[None])

    keep = keep + swap(send, "col", 1).astype(jnp.float32)
    bit = 2
    while bit < n_col:
        side = lax.axis_index("col") // bit % 2
        pairs = keep.reshape(-1, 2, per, block, columns)
        mine = lax.dynamic_index_in_dim(pairs, side, 1, keepdims=False)
        theirs = lax.dynamic_index_in_dim(pairs, 1 - side, 1, keepdims=False)
        keep = mine + swap(theirs.astype(jnp.bfloat16), "col", bit).astype(jnp.float32)
        bit *= 2
    return keep.reshape(per * block, columns).astype(jnp.bfloat16)


def solution(mesh):
    in_specs = (
        P("leaf", None),
        P("leaf", "col", None, None, None),
        P("leaf", "col", None),
        P("leaf", "col", None),
        P("leaf", "col"),
    )
    out_specs = P(("leaf", "col"), None)
    return jax.shard_map(body, mesh=mesh, in_specs=in_specs, out_specs=out_specs, check_vma=False)
```

time: 217 us -> 64.2 us (0.30)
  other arithmetic: 59.7 us -> 5.14 us
  waiting for transfers between devices: 71.1 us -> 26.4 us
  local copies, waits for them, and re-layouts: 44.3 us -> 7.77 us
  matrix products: 19.7 us -> 0 us
  between operations: 14.3 us -> 0.77 us
  Pallas kernels: 0 us -> 10.3 us
  starting transfers between devices: 7.25 us -> 13.8 us
    scatter-add x2 -> x0, other arithmetic: 56 us -> none  [the longest x1 28.3 us: body(): terms = jnp.zeros((row_blocks, block_size, columns), jnp.float32).at[bloc...]
    reduce_scatter x1 -> x0, waiting for transfers between devices: 32.4 us -> none  [body(): lax.psum_scatter(terms, 'col', scatter_dimension=0, tiled=True)]
    mul x2 -> x0, local copies, waits for them, and re-layouts: 25.1 us -> none  [the longest x1 12.6 us: body(): products * alive_weight]
    dot_general x2 -> x0, matrix products: 19.7 us -> none  [the longest x1 9.84 us: body(): jnp.einsum('kab,kbc->kac', blocks, gathered, preferred_element_type=jnp.f...]
    gather x2 -> x0, local copies, waits for them, and re-layouts: 14.2 us -> none  [the longest x1 7.21 us: body(): picked = rhs_blocks[block_rows]]
    ppermute x3 -> x5, waiting for transfers between devices: 38.7 us -> 26.4 us  [swap(): lax.ppermute(x, axis, [(i, i ^ bit) for i in range(lax.axis_size(axis))])]
    pallas_call x0 -> x2, Pallas kernels: none -> 10.3 us  [the longest x1 5.31 us: body(): pl.pallas_call(image_kernel, out_shape=(jax.ShapeDtypeStruct((n_col // 2,...]
    ppermute x3 -> x5, starting transfers between devices: 7.25 us -> 13.8 us  [swap(): lax.ppermute(x, axis, [(i, i ^ bit) for i in range(lax.axis_size(axis))])]
  transfers between devices with their start and end apart: 4 -> 5, of which waited for: 4 -> 5; matrix products, arithmetic and copies ran while one was open for 0% -> 2% of each run, Pallas kernels for 0% -> 0%
where the time goes in v1:
time: 64.2 us
  waiting for transfers between devices  26.4 us (41%)
  starting transfers between devices  13.8 us (21%)
  Pallas kernels  10.3 us (16%)
  local copies, waits for them, and re-layouts  7.77 us (12%)
  other arithmetic  5.14 us (8%)
  between operations  0.77 us (1%)
    ppermute x5, waiting for transfers between devices, swap(): lax.ppermute(x, axis, [(i, i ^ bit) for i in range(lax.axis_size(axis))])  26.4 us
    ppermute x5, starting transfers between devices, swap(): lax.ppermute(x, axis, [(i, i ^ bit) for i in range(lax.axis_size(axis))])  13.8 us
    unnamed x18, local copies, waits for them, and re-layouts  5.41 us
    pallas_call x1, Pallas kernels, body(): pl.pallas_call(image_kernel, out_shape=(jax.ShapeDtypeStruct((n_col // 2,...  5.31 us
    pallas_call x1, Pallas kernels, body(): pl.pallas_call(gather_kernel, out_shape=(jax.ShapeDtypeStruct((slots, blo...  4.96 us
    convert_element_type x3, other arithmetic, body(): both = own.astype(jnp.bfloat16)  2 us
    slice x1, local copies, waits for them, and re-layouts, body(): done = [half[:CI]]  1.55 us
    add x1, other arithmetic, body(): keep = keep + swap(send, 'col', 1).astype(jnp.float32)  1.35 us
  transfers between devices with their start and end apart: 5, of which 5 were waited for; matrix products, arithmetic and copies ran while one was open for 2% of the time, Pallas kernels for 0%

profile of v1, /device:TPU:0, one launch (start us, length us, event | category | flops | bytes accessed | tf_op | source)
XLA Modules:
  0.0 64.2 jit_solution(6861736015174612328)
XLA Ops:
  0.7 0.0 copy-start
  0.7 1.9 %copy-done = bf16[1,1,96,128,128]{4,3,2,1,0:T(8,128)(2,1)S(1)} copy-done((bf16[1,1,96,128,128]{4,3,2,1,0:T(8,128)(2,1)S(1)}, bf16[1,1,96,128,128]{4,3,2,1,0:T(8,128)(2,1)}, u32[]{:S(2)}) %copy-start) | copy-done | bytes 3145752
  2.5 0.0 copy-start.2
  2.5 1.2 %copy-done.2 = bf16[2048,256]{1,0:T(8,128)(2,1)S(1)} copy-done((bf16[2048,256]{1,0:T(8,128)(2,1)S(1)}, bf16[2048,256]{1,0:T(8,128)(2,1)}, u32[]{:S(2)}) %copy-start.2) | copy-done | bytes 1048600
  3.8 0.7 %copy-done.5 = s32[1,1,96]{2,1,0:T(1,128)S(1)} copy-done((s32[1,1,96]{2,1,0:T(1,128)S(1)}, s32[1,1,96]{2,1,0:T(1,128)}, u32[]{:S(2)}) %copy-start.5) | copy-done | bytes 408
  4.4 0.7 %copy-done.7 = s32[1,1,96]{2,1,0:T(1,128)S(1)} copy-done((s32[1,1,96]{2,1,0:T(1,128)S(1)}, s32[1,1,96]{2,1,0:T(1,128)}, u32[]{:S(2)}) %copy-start.7) | copy-done | bytes 408
  5.1 5.0 %shard_map.55 = (f32[8,128,256]{2,1,0:T(8,128)S(1)}, bf16[8,128,256]{2,1,0:T(8,128)(2,1)S(1)}) custom-call(bf16[2048,256]{1,0:T(8,128)(2,1)S(1)} %copy-done.2, bf16[96,128,128]{2,1,0:T(8,128)(2,1)S(1)} %bitcast.8, s32[96]{0:T(128)S(1)} %bitcast.10, s32[96]{0:T(128)S(1)} %bitcast.12, s32[1]{0:T(128)} %bitcast.6.count_ref), custom_call_target="tpu_custom_call" | custom-call | tf_op jit(solution)/shard_map/pallas_call | solution.py:76
  10.1 0.0 copy-start.4
  10.1 2.5 %collective-permute-start = (bf16[6,128,256]{2,1,0:T(8,128)(2,1)S(1)}, bf16[6,128,256]{2,1,0:T(8,128)(2,1)S(1)}, u32[]{:S(2)}, u32[]{:S(2)}) collective-permute-start(bf16[6,128,256]{2,1,0:T(8,128)(2,1)S(1)} %slice.29), channel_id=1, source_target_pairs={{0,4},{4,0},{8,12},{12,8},{16,20},{20,16},{24,28},{28,24},{1,5},{5... | collective-permute-start | bytes 1179656 | tf_op jit(solution)/shard_map/ppermute | solution.py:15
  12.6 8.1 %collective-permute-done = bf16[6,128,256]{2,1,0:T(8,128)(2,1)S(1)} collective-permute-done((bf16[6,128,256]{2,1,0:T(8,128)(2,1)S(1)}, bf16[6,128,256]{2,1,0:T(8,128)(2,1)S(1)}, u32[]{:S(2)}, u32[]{:S(2)}) %collective-permute-start) | collective-permute-done | bytes 393248 | tf_op jit(solution)/shard_map/ppermute | solution.py:15
  20.7 0.1 fusion.2
  20.8 0.0 copy-done.4
  20.8 4.8 %collective-permute-start.1 = (bf16[4,128,256]{2,1,0:T(8,128)(2,1)S(1)}, bf16[4,128,256]{2,1,0:T(8,128)(2,1)S(1)}, u32[]{:S(2)}, u32[]{:S(2)}) collective-permute-start(bf16[4,128,256]{2,1,0:T(8,128)(2,1)S(1)} %slice.38), channel_id=1, source_target_pairs={{0,8},{4,12},{8,0},{12,4},{16,24},{20,28},{24,16},{28,20},{1,9},{5... | collective-permute-start | bytes 786440 | tf_op jit(solution)/shard_map/ppermute | solution.py:15
  25.6 5.8 %collective-permute-done.1 = bf16[4,128,256]{2,1,0:T(8,128)(2,1)S(1)} collective-permute-done((bf16[4,128,256]{2,1,0:T(8,128)(2,1)S(1)}, bf16[4,128,256]{2,1,0:T(8,128)(2,1)S(1)}, u32[]{:S(2)}, u32[]{:S(2)}) %collective-permute-start.1) | collective-permute-done | bytes 262176 | tf_op jit(solution)/shard_map/ppermute | solution.py:15
  31.4 0.9 %fusion.1 = (bf16[4,128,256]{2,1,0:T(8,128)(2,1)S(1)}, f32[4,128,256]{2,1,0:T(8,128)}) fusion(bf16[4,128,256]{2,1,0:T(8,128)(2,1)S(1)} %collective-permute-done.1, f32[6,128,256]{2,1,0:T(8,128)S(1)} %get-tuple-element.16), kind=kLoop, calls=%fused_computation.8 | loop fusion | flops 393216 | bytes 1572864 | tf_op jit(solution)/shard_map/convert_element_type | solution.py:92
  32.2 0.7 %fusion.3 = (bf16[2,128,256]{2,1,0:T(8,128)(2,1)}, bf16[2,128,256]{2,1,0:T(8,128)(2,1)}) fusion(bf16[4,128,256]{2,1,0:T(8,128)(2,1)S(1)} %get-tuple-element.13), kind=kLoop, calls=%fused_computation.10 | loop fusion | bytes 524288 | tf_op jit(solution)/shard_map/slice | solution.py:93
  33.0 2.6 %collective-permute-start.2 = (bf16[2,128,256]{2,1,0:T(8,128)(2,1)}, bf16[2,128,256]{2,1,0:T(8,128)(2,1)}, u32[]{:S(2)}, u32[]{:S(2)}) collective-permute-start(bf16[2,128,256]{2,1,0:T(8,128)(2,1)} %get-tuple-element.18), channel_id=1, source_target_pairs={{0,16},{4,20},{8,24},{12,28},{16,0},{20,4},{24,8},{28,12},{1,17},{... | collective-permute-start | bytes 393224 | tf_op jit(solution)/shard_map/ppermute | solution.py:15
  35.6 1.5 %slice.27 = bf16[2,128,256]{2,1,0:T(8,128)(2,1)} slice(bf16[8,128,256]{2,1,0:T(8,128)(2,1)} %copy-done.4), slice={[0:2], [0:128], [0:256]} | slice | bytes 262144 | tf_op jit(solution)/shard_map/slice | solution.py:88
  37.2 3.9 %collective-permute-done.2 = bf16[2,128,256]{2,1,0:T(8,128)(2,1)} collective-permute-done((bf16[2,128,256]{2,1,0:T(8,128)(2,1)}, bf16[2,128,256]{2,1,0:T(8,128)(2,1)}, u32[]{:S(2)}, u32[]{:S(2)}) %collective-permute-start.2) | collective-permute-done | bytes 131104 | tf_op jit(solution)/shard_map/ppermute | solution.py:15
  41.0 1.0 %fusion = bf16[2,128,256]{2,1,0:T(8,128)(2,1)S(1)} fusion(f32[4,128,256]{2,1,0:T(8,128)} %get-tuple-element.14, bf16[2,128,256]{2,1,0:T(8,128)(2,1)} %collective-permute-done.2), kind=kLoop, calls=%fused_computation.7 | loop fusion | flops 196608 | bytes 524288 | tf_op jit(solution)/shard_map/convert_element_type | solution.py:92
  42.0 1.0 %pad_maximum_fusion.coarse_ref = bf16[8,128,256]{2,1,0:T(8,128)(2,1)S(1)} fusion(bf16[2,128,256]{2,1,0:T(8,128)(2,1)S(1)} %fusion, bf16[2,128,256]{2,1,0:T(8,128)(2,1)} %get-tuple-element.17, bf16[2,128,256]{2,1,0:T(8,128)(2,1)S(1)} %slice.36, bf16[2,128,256]{2,1,0:T(8,128)(2,1)} %slice.27), kind=kLoop, calls=%fused_computation.3 | loop fusion | flops 786432 | bytes 1048576 | tf_op jit(solution)/shard_map/concatenate | solution.py:95
  43.1 0.0 copy-done.1
  43.1 0.0 copy-done.6
  43.1 0.0 copy-done.8
  43.1 5.3 %shard_map.56 = (f32[2,4,128,256]{3,2,1,0:T(8,128)S(1)}, bf16[2,4,128,256]{3,2,1,0:T(8,128)(2,1)}) custom-call(bf16[8,128,256]{2,1,0:T(8,128)(2,1)S(1)} %pad_maximum_fusion.coarse_ref, bf16[96,128,128]{2,1,0:T(8,128)(2,1)S(1)} %bitcast.9, s32[96]{0:T(128)S(1)} %bitcast.11, s32[96]{0:T(128)S(1)} %bitcast.13, s32[1]{0:T(128)} %bitcast.7.count_ref, ...), custom_call_target="tpu_custom_call" | custom-call | tf_op jit(solution)/shard_map/pallas_call | solution.py:99
  48.4 1.0 %copy-done.3 = f32[2,4,128,256]{3,2,1,0:T(8,128)} copy-done((f32[2,4,128,256]{3,2,1,0:T(8,128)}, f32[2,4,128,256]{3,2,1,0:T(8,128)S(1)}, u32[]{:S(2)}) %copy-start.3) | copy-done | bytes 1048600
  49.4 0.0 collective-permute-start.3
  49.4 2.1 %collective-permute-done.3 = bf16[2,4,128,256]{3,2,1,0:T(8,128)(2,1)S(1)} collective-permute-done((bf16[2,4,128,256]{3,2,1,0:T(8,128)(2,1)}, bf16[2,4,128,256]{3,2,1,0:T(8,128)(2,1)S(1)}, u32[]{:S(2)}, u32[]{:S(2)}) %collective-permute-start.3) | collective-permute-done | bytes 524320 | tf_op jit(solution)/shard_map/ppermute | solution.py:15
  51.5 1.3 %convert_add_fusion = f32[2,4,128,256]{3,2,1,0:T(8,128)S(1)} fusion(f32[2,4,128,256]{3,2,1,0:T(8,128)} %copy-done.3, bf16[2,4,128,256]{3,2,1,0:T(8,128)(2,1)S(1)} %collective-permute-done.3), kind=kLoop, calls=%fused_computation | loop fusion | flops 524288 | bytes 2621440 | tf_op jit(solution)/shard_map/add | solution.py:111
  52.9 3.9 %collective-permute-start.4 = (bf16[1,4,128,256]{3,2,1,0:T(8,128)(2,1)S(1)}, bf16[1,4,128,256]{3,2,1,0:T(8,128)(2,1)S(1)}, u32[]{:S(2)}, u32[]{:S(2)}) collective-permute-start(bf16[1,4,128,256]{3,2,1,0:T(8,128)(2,1)S(1)} %dynamic-slice_convert_fusion), channel_id=1, source_target_pairs={{0,2},{1,3},{2,0},{3,1},{4,6},{5,7},{6,4},{7,5},{8,10},{9,11},{10,... | collective-permute-start | bytes 786440 | tf_op jit(solution)/shard_map/ppermute | solution.py:15
  56.9 6.6 %collective-permute-done.4 = bf16[1,4,128,256]{3,2,1,0:T(8,128)(2,1)S(1)} collective-permute-done((bf16[1,4,128,256]{3,2,1,0:T(8,128)(2,1)S(1)}, bf16[1,4,128,256]{3,2,1,0:T(8,128)(2,1)S(1)}, u32[]{:S(2)}, u32[]{:S(2)}) %collective-permute-start.4) | collective-permute-done | bytes 262176 | tf_op jit(solution)/shard_map/ppermute | solution.py:15
  63.5 0.8 %add_convert_fusion = bf16[1,4,128,256]{3,2,1,0:T(8,128)(2,1)} fusion(bf16[1,4,128,256]{3,2,1,0:T(8,128)(2,1)S(1)} %collective-permute-done.4, f32[2,4,128,256]{3,2,1,0:T(8,128)S(1)} %convert_add_fusion, s32[]{:T(128)S(6)} %select_n.25), kind=kLoop, calls=%fused_computation.4 | loop fusion | flops 393216 | bytes 1048580 | tf_op jit(solution)/shard_map/convert_element_type | solution.py:120
  (10 shorter events, 0.1 us)
Async XLA Ops:
  0.7 1.9 %copy-start = (bf16[1,1,96,128,128]{4,3,2,1,0:T(8,128)(2,1)S(1)}, bf16[1,1,96,128,128]{4,3,2,1,0:T(8,128)(2,1)}, u32[]{:S(2)}) copy-start(bf16[1,1,96,128,128]{4,3,2,1,0:T(8,128)(2,1)} %param.6) | copy-start | bytes 9437188
  2.5 1.2 %copy-start.2 = (bf16[2048,256]{1,0:T(8,128)(2,1)S(1)}, bf16[2048,256]{1,0:T(8,128)(2,1)}, u32[]{:S(2)}) copy-start(bf16[2048,256]{1,0:T(8,128)(2,1)} %rhs_ref.1) | copy-start | bytes 3145732
  3.8 0.7 %copy-start.5 = (s32[1,1,96]{2,1,0:T(1,128)S(1)}, s32[1,1,96]{2,1,0:T(1,128)}, u32[]{:S(2)}) copy-start(s32[1,1,96]{2,1,0:T(1,128)} %param.7) | copy-start | bytes 1156
  4.4 0.7 %copy-start.7 = (s32[1,1,96]{2,1,0:T(1,128)S(1)}, s32[1,1,96]{2,1,0:T(1,128)}, u32[]{:S(2)}) copy-start(s32[1,1,96]{2,1,0:T(1,128)} %param.8) | copy-start | bytes 1156
  10.1 10.8 %copy-start.4 = (bf16[8,128,256]{2,1,0:T(8,128)(2,1)}, bf16[8,128,256]{2,1,0:T(8,128)(2,1)S(1)}, u32[]{:S(2)}) copy-start(bf16[8,128,256]{2,1,0:T(8,128)(2,1)S(1)} %get-tuple-element.9) | copy-start | bytes 1572868
  10.1 10.6 %collective-permute-start = (bf16[6,128,256]{2,1,0:T(8,128)(2,1)S(1)}, bf16[6,128,256]{2,1,0:T(8,128)(2,1)S(1)}, u32[]{:S(2)}, u32[]{:S(2)}) collective-permute-start(bf16[6,128,256]{2,1,0:T(8,128)(2,1)S(1)} %slice.29), channel_id=1, source_target_pairs={{0,4},{4,0},{8,12},{12,8},{16,20},{20,16},{24,28},{28,24},{1,5},{5... | collective-permute-start | bytes 1179656 | tf_op jit(solution)/shard_map/ppermute | solution.py:15
  20.7 22.4 %copy-start.1 = (bf16[1,1,96,128,128]{4,3,2,1,0:T(8,128)(2,1)S(1)}, bf16[1,1,96,128,128]{4,3,2,1,0:T(8,128)(2,1)}, u32[]{:S(2)}) copy-start(bf16[1,1,96,128,128]{4,3,2,1,0:T(8,128)(2,1)} %param.6) | copy-start | bytes 9437188
  20.7 22.4 %copy-start.6 = (s32[1,1,96]{2,1,0:T(1,128)S(1)}, s32[1,1,96]{2,1,0:T(1,128)}, u32[]{:S(2)}) copy-start(s32[1,1,96]{2,1,0:T(1,128)} %param.7) | copy-start | bytes 1156
  20.7 22.4 %copy-start.8 = (s32[1,1,96]{2,1,0:T(1,128)S(1)}, s32[1,1,96]{2,1,0:T(1,128)}, u32[]{:S(2)}) copy-start(s32[1,1,96]{2,1,0:T(1,128)} %param.8) | copy-start | bytes 1156
  20.8 10.5 %collective-permute-start.1 = (bf16[4,128,256]{2,1,0:T(8,128)(2,1)S(1)}, bf16[4,128,256]{2,1,0:T(8,128)(2,1)S(1)}, u32[]{:S(2)}, u32[]{:S(2)}) collective-permute-start(bf16[4,128,256]{2,1,0:T(8,128)(2,1)S(1)} %slice.38), channel_id=1, source_target_pairs={{0,8},{4,12},{8,0},{12,4},{16,24},{20,28},{24,16},{28,20},{1,9},{5... | collective-permute-start | bytes 786440 | tf_op jit(solution)/shard_map/ppermute | solution.py:15
  33.0 8.1 %collective-permute-start.2 = (bf16[2,128,256]{2,1,0:T(8,128)(2,1)}, bf16[2,128,256]{2,1,0:T(8,128)(2,1)}, u32[]{:S(2)}, u32[]{:S(2)}) collective-permute-start(bf16[2,128,256]{2,1,0:T(8,128)(2,1)} %get-tuple-element.18), channel_id=1, source_target_pairs={{0,16},{4,20},{8,24},{12,28},{16,0},{20,4},{24,8},{28,12},{1,17},{... | collective-permute-start | bytes 393224 | tf_op jit(solution)/shard_map/ppermute | solution.py:15
  48.4 1.0 %copy-start.3 = (f32[2,4,128,256]{3,2,1,0:T(8,128)}, f32[2,4,128,256]{3,2,1,0:T(8,128)S(1)}, u32[]{:S(2)}) copy-start(f32[2,4,128,256]{3,2,1,0:T(8,128)S(1)} %get-tuple-element.11) | copy-start | bytes 3145732
  49.4 2.1 %collective-permute-start.3 = (bf16[2,4,128,256]{3,2,1,0:T(8,128)(2,1)}, bf16[2,4,128,256]{3,2,1,0:T(8,128)(2,1)S(1)}, u32[]{:S(2)}, u32[]{:S(2)}) collective-permute-start(bf16[2,4,128,256]{3,2,1,0:T(8,128)(2,1)} %get-tuple-element.12), channel_id=1, source_target_pairs={{0,1},{1,0},{2,3},{3,2},{4,5},{5,4},{6,7},{7,6},{8,9},{9,8},{10,11... | collective-permute-start | bytes 1572872 | tf_op jit(solution)/shard_map/ppermute | solution.py:15
  52.9 10.6 %collective-permute-start.4 = (bf16[1,4,128,256]{3,2,1,0:T(8,128)(2,1)S(1)}, bf16[1,4,128,256]{3,2,1,0:T(8,128)(2,1)S(1)}, u32[]{:S(2)}, u32[]{:S(2)}) collective-permute-start(bf16[1,4,128,256]{3,2,1,0:T(8,128)(2,1)S(1)} %dynamic-slice_convert_fusion), channel_id=1, source_target_pairs={{0,2},{1,3},{2,0},{3,1},{4,6},{5,7},{6,4},{7,5},{8,10},{9,11},{10,... | collective-permute-start | bytes 786440 | tf_op jit(solution)/shard_map/ppermute | solution.py:15

commit v2 on v0

v2 whole, which is shorter than its diff:
```python
import functools

import jax
import jax.numpy as jnp
from jax import lax
from jax.experimental import pallas as pl
from jax.experimental.pallas import tpu as pltpu
from jax.sharding import PartitionSpec as P

CI = 2
SEP = 2
BODIES = (24, 8)
CHUNKS = 4
BITS = 10
VMEM_LIMIT = 8 << 20

F32 = jnp.float32
BF16 = jnp.bfloat16
VMEM = pl.BlockSpec(memory_space=pltpu.VMEM)
ANY = pl.BlockSpec(memory_space=pl.ANY)
TOP, REST, FOUND = 0, 1, 2


def swap(x, axis, bits):
    return lax.ppermute(x, axis, [(i, i ^ bits) for i in range(lax.axis_size(axis))])


def over_list(plan_ref, which, one):
    found = plan_ref[FOUND, which]
    mask = (1 << BITS) - 1

    def body(size):
        def group(j, base):
            for u in range(size):
                at = base + u
                entry = plan_ref[which, jnp.minimum(at, found - 1)]
                one(entry & mask, (entry >> BITS) & mask, entry >> (2 * BITS), at < found)
            return base + size

        return group

    base = jnp.int32(0)
    for size in BODIES[:-1]:
        base = lax.fori_loop(0, (found - base) // size, body(size), base)
    size = BODIES[-1]
    lax.fori_loop(0, (found - base + size - 1) // size, body(size), base)


def project(which, low, plan_ref, x_ref, rhs_ref, acc_ref):
    block = x_ref.shape[1]
    trash = acc_ref.shape[0] - 1

    def one(k, row, col, used):
        at = pl.multiple_of(row * block, block)
        acc_ref[jnp.where(used, col - low, trash)] += lax.dot_general(
            x_ref[k], rhs_ref[pl.ds(at, block), :], (((0,), (0,)), ((), ())), preferred_element_type=F32
        )

    over_list(plan_ref, which, one)


def image(which, low, per, flip, plan_ref, x_ref, coarse_ref, acc_ref):
    trash = acc_ref.shape[0] - 1

    def one(k, row, col, used):
        at = ((row // per) ^ flip) * per + row % per
        acc_ref[jnp.where(used, at, trash)] += jnp.dot(x_ref[k], coarse_ref[col - low], preferred_element_type=F32)

    over_list(plan_ref, which, one)


def first_kernel(low, x_hbm, rhs_hbm, row_hbm, col_hbm, count_hbm, x_ref, rhs_ref, part_ref, half_ref, plan_out,
                 row_ref, col_ref, count_ref, plan_ref, acc_ref, id_sem, big_sem):
    list_len = x_ref.shape[0]
    per = list_len // CHUNKS
    ids = [
        pltpu.make_async_copy(row_hbm, row_ref, id_sem.at[0]),
        pltpu.make_async_copy(col_hbm, col_ref, id_sem.at[1]),
        pltpu.make_async_copy(count_hbm, count_ref, id_sem.at[2]),
    ]
    big = [
        pltpu.make_async_copy(x_hbm.at[pl.ds(i * per, per)], x_ref.at[pl.ds(i * per, per)], big_sem.at[i])
        for i in range(CHUNKS)
    ]
    big.append(pltpu.make_async_copy(rhs_hbm, rhs_ref, big_sem.at[CHUNKS]))
    for copy in ids + big:
        copy.start()
    acc_ref[...] = jnp.zeros_like(acc_ref)
    for copy in ids:
        copy.wait()

    def scan(j, found):
        top, rest = found
        for u in range(8):
            k = j * 8 + u
            col = col_ref[k]
            entry = k + (row_ref[k] << BITS) + (col << (2 * BITS))
            used = k < count_ref[0]
            plan_ref[TOP, top] = entry
            plan_ref[REST, rest] = entry
            top += (used & (col >= low)).astype(jnp.int32)
            rest += (used & (col < low)).astype(jnp.int32)
        return top, rest

    top, rest = lax.fori_loop(0, list_len // 8, scan, (jnp.int32(0), jnp.int32(0)))
    plan_ref[FOUND, TOP] = top
    plan_ref[FOUND, REST] = rest
    out = pltpu.make_async_copy(plan_ref, plan_out, id_sem.at[3])
    out.start()
    for copy in big:
        copy.wait()
    project(TOP, low, plan_ref, x_ref, rhs_ref, acc_ref)
    for c in range(part_ref.shape[0]):
        part_ref[c] = acc_ref[c]
        half_ref[c] = acc_ref[c].astype(BF16)
    out.wait()


def rest_kernel(plan_hbm, x_ref, rhs_ref, _, inner_ref, *refs):
    outs, (plan_ref, acc_ref, sem) = refs[:-3], refs[-3:]
    copy = pltpu.make_async_copy(plan_hbm, plan_ref, sem)
    copy.start()
    acc_ref[...] = jnp.zeros_like(acc_ref)
    copy.wait()
    project(REST, 0, plan_ref, x_ref, rhs_ref, acc_ref)
    for c in range(CI):
        inner_ref[c] = acc_ref[c].astype(BF16)
    for n in range(len(outs) // 2):
        part_ref, half_ref = outs[2 * n : 2 * n + 2]
        for c in range(SEP):
            part_ref[c] = acc_ref[CI + n * SEP + c]
            half_ref[c] = acc_ref[CI + n * SEP + c].astype(BF16)


def add_kernel(own_ref, got_ref, *refs):
    sum_ref, half_ref = refs[-2:]
    total = own_ref[...] + got_ref[...].astype(F32)
    sum_ref[...] = total
    half_ref[...] = total.astype(BF16)


def mid_kernel(per, plan_hbm, x_ref, inner_ref, *refs):
    sums, (acc_ref, plan_ref, coarse_ref, sem) = refs[:-5], refs[-4:]
    copy = pltpu.make_async_copy(plan_hbm, plan_ref, sem)
    copy.start()
    acc_ref[...] = jnp.zeros_like(acc_ref)
    coarse_ref[:CI] = inner_ref[...]
    for n in range(len(sums) // 2):
        own_ref, got_ref = sums[2 * n : 2 * n + 2]
        coarse_ref[CI + n * SEP : CI + (n + 1) * SEP] = (own_ref[...] + got_ref[...].astype(F32)).astype(BF16)
    copy.wait()
    image(REST, 0, per, lax.axis_index("col"), plan_ref, x_ref, coarse_ref, acc_ref)


def last_kernel(low, per, plan_hbm, x_ref, own_ref, got_ref, old_ref, acc_ref, keep_ref, send_ref, plan_ref, coarse_ref, sem):
    copy = pltpu.make_async_copy(plan_hbm, plan_ref, sem)
    copy.start()
    coarse_ref[...] = (own_ref[...] + got_ref[...].astype(F32)).astype(BF16)
    copy.wait()
    image(TOP, low, per, lax.axis_index("col"), plan_ref, x_ref, coarse_ref, acc_ref)
    for g in range(keep_ref.shape[0]):
        for b in range(per):
            send_ref[g, b] = acc_ref[(2 * g + 1) * per + b].astype(BF16)
            keep_ref[g, b] = acc_ref[2 * g * per + b]


def body(right_side, x_blocks, row_ids, col_ids, counts):
    blocks, rows, cols, count = x_blocks[0, 0], row_ids[0, 0], col_ids[0, 0], counts[0]
    list_len, block, _ = blocks.shape
    columns = right_side.shape[1]
    row_blocks = right_side.shape[0] // block
    levels = lax.axis_size("leaf").bit_length() - 1
    n_col = lax.axis_size("col")
    per = row_blocks // n_col
    slots = CI + levels * SEP
    low = slots - SEP
    params = pltpu.CompilerParams(vmem_limit_bytes=VMEM_LIMIT)
    free = pl.CostEstimate(flops=0, bytes_accessed=0, transcendentals=0)

    def tiles(n, dtype):
        return pltpu.VMEM((n, block, columns), dtype)

    def in_vmem(*arrays):
        return [pltpu.with_memory_space_constraint(a, pltpu.VMEM) for a in arrays]

    def in_hbm(*arrays):
        return [pltpu.with_memory_space_constraint(a, pltpu.HBM) for a in arrays]

    plan_shape = (8, (list_len + 128) // 128 * 128)
    plan_scratch = pltpu.SMEM(plan_shape, jnp.int32)
    pair = (tiles(SEP, F32), tiles(SEP, BF16))
    sem = pltpu.SemaphoreType.DMA

    x_vmem, rhs_vmem, part, half, plan = pl.pallas_call(
        functools.partial(first_kernel, low),
        out_shape=(pltpu.VMEM(blocks.shape, BF16), pltpu.VMEM(right_side.shape, BF16), *pair, pltpu.VMEM(plan_shape, jnp.int32)),
        in_specs=[ANY] * 5,
        out_specs=(VMEM,) * 5,
        scratch_shapes=[
            pltpu.SMEM((list_len,), jnp.int32),
            pltpu.SMEM((list_len,), jnp.int32),
            pltpu.SMEM((1,), jnp.int32),
            plan_scratch,
            tiles(SEP + 1, F32),
            sem((4,)),
            sem((CHUNKS + 1,)),
        ],
        compiler_params=params,
        cost_estimate=free,
    )(*in_hbm(blocks, right_side, rows, cols), count)
    own, sent, got = {levels: part}, {levels: half}, {}

    def exchange(level, step):
        bits = (2 << step) - 2 if step > 1 else 1 << step
        got[level] = swap(sent[level], "leaf", bits)

    def add(level, *alive):
        own[level], sent[level] = pl.pallas_call(
            add_kernel,
            out_shape=pair,
            in_specs=[VMEM] * (2 + len(alive)),
            out_specs=(VMEM,) * 2,
            compiler_params=params,
            cost_estimate=free,
        )(*in_vmem(own[level], got[level], *alive))

    inner, *others = pl.pallas_call(
        rest_kernel,
        out_shape=(tiles(CI, BF16), *pair * (levels - 1)),
        in_specs=[VMEM] * 4,
        out_specs=(VMEM,) * (2 * levels - 1),
        scratch_shapes=[plan_scratch, tiles(low + 1, F32), sem(())],
        compiler_params=params,
        cost_estimate=free,
    )(*in_vmem(plan, x_vmem, rhs_vmem, own[levels]))
    for n in range(levels - 1):
        own[n + 1], sent[n + 1] = others[2 * n : 2 * n + 2]

    for step in range(levels):
        for level in range(levels, step, -1):
            exchange(level, step)
            if level > step + 1:
                add(level, x_vmem, inner, *[own[n] for n in range(1, levels) if n != level])

    sums = [array for level in range(1, levels) for array in (own[level], got[level])]
    terms = pl.pallas_call(
        functools.partial(mid_kernel, per),
        out_shape=tiles(row_blocks + 1, F32),
        in_specs=[VMEM] * (4 + len(sums)),
        out_specs=VMEM,
        scratch_shapes=[plan_scratch, tiles(low, BF16), sem(())],
        compiler_params=params,
        cost_estimate=free,
    )(*in_vmem(plan, x_vmem, inner, *sums, own[levels]))

    _, keep, send = pl.pallas_call(
        functools.partial(last_kernel, low, per),
        out_shape=(
            tiles(row_blocks + 1, F32),
            pltpu.VMEM((n_col // 2, per, block, columns), F32),
            pltpu.VMEM((n_col // 2, per, block, columns), BF16),
        ),
        in_specs=[VMEM] * 5,
        out_specs=(VMEM,) * 3,
        scratch_shapes=[plan_scratch, tiles(SEP, BF16), sem(())],
        input_output_aliases={4: 0},
        compiler_params=params,
        cost_estimate=free,
    )(*in_vmem(plan, x_vmem, own[levels], got[levels], terms))

    bit = 1
    while True:
        keep = keep + swap(send, "col", bit).astype(F32)
        bit *= 2
        if bit == n_col:
            return keep.reshape(per * block, columns).astype(BF16)
        pairs = keep.reshape(-1, 2, per, block, columns)
        keep, send = pairs[:, 0], pairs[:, 1].astype(BF16)


def solution(mesh):
    in_specs = (
        P("leaf", None),
        P("leaf", "col", None, None, None),
        P("leaf", "col", None),
        P("leaf", "col", None),
        P("leaf", "col"),
    )
    out_specs = P(("leaf", "col"), None)
    return jax.shard_map(body, mesh=mesh, in_specs=in_specs, out_specs=out_specs, check_vma=False)
```

time: 217 us -> 37.9 us (0.17)
  other arithmetic: 59.7 us -> 0.9 us
  waiting for transfers between devices: 71.1 us -> 13.9 us
  local copies, waits for them, and re-layouts: 44.3 us -> 0.03 us
  matrix products: 19.7 us -> 0 us
  between operations: 14.3 us -> 0.72 us
  Pallas kernels: 0 us -> 8.98 us
  starting transfers between devices: 7.25 us -> 13 us
    scatter-add x2 -> x0, other arithmetic: 56 us -> none  [the longest x1 28.3 us: body(): terms = jnp.zeros((row_blocks, block_size, columns), jnp.float32).at[bloc...]
    reduce_scatter x1 -> x0, waiting for transfers between devices: 32.4 us -> none  [body(): lax.psum_scatter(terms, 'col', scatter_dimension=0, tiled=True)]
    mul x2 -> x0, local copies, waits for them, and re-layouts: 25.1 us -> none  [the longest x1 12.6 us: body(): products * alive_weight]
    ppermute x3 -> x8, waiting for transfers between devices: 38.7 us -> 13.9 us  [swap(): lax.ppermute(x, axis, [(i, i ^ bits) for i in range(lax.axis_size(axis))])]
    dot_general x2 -> x0, matrix products: 19.7 us -> none  [the longest x1 9.84 us: body(): jnp.einsum('kab,kbc->kac', blocks, gathered, preferred_element_type=jnp.f...]
    gather x2 -> x0, local copies, waits for them, and re-layouts: 14.2 us -> none  [the longest x1 7.21 us: body(): picked = rhs_blocks[block_rows]]
    pallas_call x0 -> x7, Pallas kernels: none -> 8.98 us  [the longest x1 2.97 us: body(): pl.pallas_call(functools.partial(first_kernel, low), out_shape=(pltpu.VME...]
    ppermute x3 -> x8, starting transfers between devices: 7.25 us -> 13 us  [swap(): lax.ppermute(x, axis, [(i, i ^ bits) for i in range(lax.axis_size(axis))])]
  transfers between devices with their start and end apart: 4 -> 8, of which waited for: 4 -> 6; matrix products, arithmetic and copies ran while one was open for 0% -> 0% of each run, Pallas kernels for 0% -> 12%
where the time goes in v2:
time: 37.9 us; the launch traced here: 37.6 us
  waiting for transfers between devices  13.9 us (37%)
  starting transfers between devices  13 us (34%)
  Pallas kernels  8.98 us (24%)
  other arithmetic  0.9 us (2%)
  between operations  0.72 us (2%)
    ppermute x8, waiting for transfers between devices, swap(): lax.ppermute(x, axis, [(i, i ^ bits) for i in range(lax.axis_size(axis))])  13.9 us
    ppermute x8, starting transfers between devices, swap(): lax.ppermute(x, axis, [(i, i ^ bits) for i in range(lax.axis_size(axis))])  13 us
    pallas_call x1, Pallas kernels, body(): pl.pallas_call(functools.partial(first_kernel, low), out_shape=(pltpu.VME...  2.97 us
    pallas_call x1, Pallas kernels, body(): pl.pallas_call(rest_kernel, out_shape=(tiles(CI, BF16), *pair * (levels -...  2.37 us
    pallas_call x1, Pallas kernels, body(): pl.pallas_call(functools.partial(mid_kernel, per), out_shape=tiles(row_bl...  2.16 us
    pallas_call x1, Pallas kernels, body(): pl.pallas_call(functools.partial(last_kernel, low, per), out_shape=(tiles...  1.37 us
    convert_element_type x1, other arithmetic, body(): return keep.reshape(per * block, columns).astype(BF16)  0.78 us
  transfers between devices with their start and end apart: 8, of which 6 were waited for; matrix products, arithmetic and copies ran while one was open for 0% of the time, Pallas kernels for 12%

profile of v2, /device:TPU:0, one launch (start us, length us, event | category | flops | bytes accessed | tf_op | source)
XLA Modules:
  0.0 37.6 jit_solution(4570820172079483829)
XLA Ops:
  0.7 3.0 %shard_map.55 = (bf16[96,128,128]{2,1,0:T(8,128)(2,1)S(1)}, bf16[2048,256]{1,0:T(8,128)(2,1)S(1)}, f32[2,128,256]{2,1,0:T(8,128)S(1)}, bf16[2,128,256]{2,1,0:T(8,128)(2,1)S(1)}, s32[8,128]{1,0:T(8,128)S(1)}) custom-call(bf16[96,128,128]{2,1,0:T(8,128)(2,1)} %bitcast.16, bf16[2048,256]{1,0:T(8,128)(2,1)} %rhs_hbm.1, s32[96]{0:T(128)} %bitcast.17, ...), custom_call_target="tpu_custom_call" | custom-call | tf_op jit(solution)/shard_map/pallas_call | solution.py:194
  3.6 3.3 %collective-permute-start = (bf16[2,128,256]{2,1,0:T(8,128)(2,1)S(1)}, bf16[2,128,256]{2,1,0:T(8,128)(2,1)S(1)}, u32[]{:S(2)}, u32[]{:S(2)}) collective-permute-start(bf16[2,128,256]{2,1,0:T(8,128)(2,1)S(1)} %get-tuple-element.26), channel_id=1, source_target_pairs={{0,4},{4,0},{8,12},{12,8},{16,20},{20,16},{24,28},{28,24},{1,5},{5... | collective-permute-start | bytes 393224 | tf_op jit(solution)/shard_map/ppermute | solution.py:25
  6.9 2.4 %shard_map.56 = (bf16[2,128,256]{2,1,0:T(8,128)(2,1)S(1)}, f32[2,128,256]{2,1,0:T(8,128)S(1)}, bf16[2,128,256]{2,1,0:T(8,128)(2,1)S(1)}, f32[2,128,256]{2,1,0:T(8,128)S(1)}, bf16[2,128,256]{2,1,0:T(8,128)(2,1)S(1)}) custom-call(s32[8,128]{1,0:T(8,128)S(1)} %get-tuple-element.23.plan_hbm, bf16[96,128,128]{2,1,0:T(8,128)(2,1)S(1)} %get-tuple-element.24.x_ref.refs_0_, ...), custom_call_target="tpu_custom_call" | custom-call | tf_op jit(solution)/shard_map/pallas_call | solution.py:227
  9.3 0.7 %collective-permute-start.2 = (bf16[2,128,256]{2,1,0:T(8,128)(2,1)S(1)}, bf16[2,128,256]{2,1,0:T(8,128)(2,1)S(1)}, u32[]{:S(2)}, u32[]{:S(2)}) collective-permute-start(bf16[2,128,256]{2,1,0:T(8,128)(2,1)S(1)} %get-tuple-element.33), channel_id=1, source_target_pairs={{0,4},{4,0},{8,12},{12,8},{16,20},{20,16},{24,28},{28,24},{1,5},{5... | collective-permute-start | bytes 393224 | tf_op jit(solution)/shard_map/ppermute | solution.py:25
  10.0 0.4 %collective-permute-done.got_ref = bf16[2,128,256]{2,1,0:T(8,128)(2,1)S(1)} collective-permute-done((bf16[2,128,256]{2,1,0:T(8,128)(2,1)S(1)}, bf16[2,128,256]{2,1,0:T(8,128)(2,1)S(1)}, u32[]{:S(2)}, u32[]{:S(2)}) %collective-permute-start) | collective-permute-done | bytes 131104 | tf_op jit(solution)/shard_map/ppermute | solution.py:25
  10.5 1.7 %collective-permute-start.1 = (bf16[2,128,256]{2,1,0:T(8,128)(2,1)S(1)}, bf16[2,128,256]{2,1,0:T(8,128)(2,1)S(1)}, u32[]{:S(2)}, u32[]{:S(2)}) collective-permute-start(bf16[2,128,256]{2,1,0:T(8,128)(2,1)S(1)} %get-tuple-element.32), channel_id=1, source_target_pairs={{0,8},{4,12},{8,0},{12,4},{16,24},{20,28},{24,16},{28,20},{1,9},{5... | collective-permute-start | bytes 393224 | tf_op jit(solution)/shard_map/ppermute | solution.py:25
  12.1 1.5 %collective-permute-start.4 = (bf16[2,128,256]{2,1,0:T(8,128)(2,1)S(1)}, bf16[2,128,256]{2,1,0:T(8,128)(2,1)S(1)}, u32[]{:S(2)}, u32[]{:S(2)}) collective-permute-start(bf16[2,128,256]{2,1,0:T(8,128)(2,1)S(1)} %get-tuple-element.37), channel_id=1, source_target_pairs={{0,4},{4,0},{8,12},{12,8},{16,20},{20,16},{24,28},{28,24},{1,5},{5... | collective-permute-start | bytes 393224 | tf_op jit(solution)/shard_map/ppermute | solution.py:25
  13.6 2.0 %collective-permute-done.2.got_ref = bf16[2,128,256]{2,1,0:T(8,128)(2,1)S(1)} collective-permute-done((bf16[2,128,256]{2,1,0:T(8,128)(2,1)S(1)}, bf16[2,128,256]{2,1,0:T(8,128)(2,1)S(1)}, u32[]{:S(2)}, u32[]{:S(2)}) %collective-permute-start.2) | collective-permute-done | bytes 131104 | tf_op jit(solution)/shard_map/ppermute | solution.py:25
  15.7 1.5 %collective-permute-start.5 = (bf16[2,128,256]{2,1,0:T(8,128)(2,1)S(1)}, bf16[2,128,256]{2,1,0:T(8,128)(2,1)S(1)}, u32[]{:S(2)}, u32[]{:S(2)}) collective-permute-start(bf16[2,128,256]{2,1,0:T(8,128)(2,1)S(1)} %get-tuple-element.38), channel_id=1, source_target_pairs={{0,8},{4,12},{8,0},{12,4},{16,24},{20,28},{24,16},{28,20},{1,9},{5... | collective-permute-start | bytes 393224 | tf_op jit(solution)/shard_map/ppermute | solution.py:25
  17.1 0.0 collective-permute-done.1.got_ref
  17.2 2.3 %collective-permute-start.3 = (bf16[2,128,256]{2,1,0:T(8,128)(2,1)S(1)}, bf16[2,128,256]{2,1,0:T(8,128)(2,1)S(1)}, u32[]{:S(2)}, u32[]{:S(2)}) collective-permute-start(bf16[2,128,256]{2,1,0:T(8,128)(2,1)S(1)} %get-tuple-element.36), channel_id=1, source_target_pairs={{0,24},{4,28},{8,16},{12,20},{16,8},{20,12},{24,0},{28,4},{1,25},{... | collective-permute-start | bytes 393224 | tf_op jit(solution)/shard_map/ppermute | solution.py:25
  19.5 0.0 collective-permute-done.4.refs_1_
  19.5 1.4 %collective-permute-done.5.refs_3_ = bf16[2,128,256]{2,1,0:T(8,128)(2,1)S(1)} collective-permute-done((bf16[2,128,256]{2,1,0:T(8,128)(2,1)S(1)}, bf16[2,128,256]{2,1,0:T(8,128)(2,1)S(1)}, u32[]{:S(2)}, u32[]{:S(2)}) %collective-permute-start.5) | collective-permute-done | bytes 131104 | tf_op jit(solution)/shard_map/ppermute | solution.py:25
  20.9 2.2 %shard_map.60.old_ref = f32[17,128,256]{2,1,0:T(8,128)S(1)} custom-call(s32[8,128]{1,0:T(8,128)S(1)} %get-tuple-element.23.plan_hbm, bf16[96,128,128]{2,1,0:T(8,128)(2,1)S(1)} %get-tuple-element.24.x_ref.refs_0_, bf16[2,128,256]{2,1,0:T(8,128)(2,1)S(1)} %get-tuple-element.28.refs_1_.inner_ref, f32[2,128,256]{2,1,0:T(8,128)S(1)} %get-tuple-element.29.refs_2_.refs_0_, ...), custom_call_target="tpu_custom_call" | custom-call | tf_op jit(solution)/shard_map/pallas_call | solution.py:246
  23.1 1.6 %collective-permute-done.3.got_ref = bf16[2,128,256]{2,1,0:T(8,128)(2,1)S(1)} collective-permute-done((bf16[2,128,256]{2,1,0:T(8,128)(2,1)S(1)}, bf16[2,128,256]{2,1,0:T(8,128)(2,1)S(1)}, u32[]{:S(2)}, u32[]{:S(2)}) %collective-permute-start.3) | collective-permute-done | bytes 131104 | tf_op jit(solution)/shard_map/ppermute | solution.py:25
  24.7 1.4 %shard_map.61 = (f32[17,128,256]{2,1,0:T(8,128)S(1)}, f32[2,4,128,256]{3,2,1,0:T(8,128)S(1)}, bf16[2,4,128,256]{3,2,1,0:T(8,128)(2,1)S(1)}) custom-call(s32[8,128]{1,0:T(8,128)S(1)} %get-tuple-element.23.plan_hbm, bf16[96,128,128]{2,1,0:T(8,128)(2,1)S(1)} %get-tuple-element.24.x_ref.refs_0_, ...), custom_call_target="tpu_custom_call", output_to_operand_aliasing={{0}: (4, {})} | custom-call | tf_op jit(solution)/shard_map/pallas_call | solution.py:256
  26.1 0.1 collective-permute-start.6
  26.2 1.9 %collective-permute-done.6 = bf16[2,4,128,256]{3,2,1,0:T(8,128)(2,1)S(1)} collective-permute-done((bf16[2,4,128,256]{3,2,1,0:T(8,128)(2,1)S(1)}, bf16[2,4,128,256]{3,2,1,0:T(8,128)(2,1)S(1)}, u32[]{:S(2)}, u32[]{:S(2)}) %collective-permute-start.6) | collective-permute-done | bytes 524320 | tf_op jit(solution)/shard_map/ppermute | solution.py:25
  28.0 0.1 add_bitcast_fusion
  28.2 2.0 %collective-permute-start.7 = (bf16[1,4,128,256]{3,2,1,0:T(8,128)(2,1)S(1)}, bf16[1,4,128,256]{3,2,1,0:T(8,128)(2,1)S(1)}, u32[]{:S(2)}, u32[]{:S(2)}) collective-permute-start(bf16[1,4,128,256]{3,2,1,0:T(8,128)(2,1)S(1)} %fusion.2), channel_id=1, source_target_pairs={{0,2},{1,3},{2,0},{3,1},{4,6},{5,7},{6,4},{7,5},{8,10},{9,11},{10,... | collective-permute-start | bytes 786440 | tf_op jit(solution)/shard_map/ppermute | solution.py:25
  30.2 6.6 %collective-permute-done.7 = bf16[1,4,128,256]{3,2,1,0:T(8,128)(2,1)S(1)} collective-permute-done((bf16[1,4,128,256]{3,2,1,0:T(8,128)(2,1)S(1)}, bf16[1,4,128,256]{3,2,1,0:T(8,128)(2,1)S(1)}, u32[]{:S(2)}, u32[]{:S(2)}) %collective-permute-start.7) | collective-permute-done | bytes 262176 | tf_op jit(solution)/shard_map/ppermute | solution.py:25
  36.8 0.8 %fusion.1 = bf16[1,4,128,256]{3,2,1,0:T(8,128)(2,1)} fusion(f32[1,2,4,128,256]{4,3,2,1,0:T(8,128)S(1)} %add_bitcast_fusion, bf16[1,4,128,256]{3,2,1,0:T(8,128)(2,1)S(1)} %collective-permute-done.7), kind=kLoop, calls=%fused_computation.4 | loop fusion | flops 393216 | bytes 1048576 | tf_op jit(solution)/shard_map/convert_element_type | solution.py:276
  (4 shorter events, 0.1 us)
Async XLA Ops:
  3.6 6.8 %collective-permute-start = (bf16[2,128,256]{2,1,0:T(8,128)(2,1)S(1)}, bf16[2,128,256]{2,1,0:T(8,128)(2,1)S(1)}, u32[]{:S(2)}, u32[]{:S(2)}) collective-permute-start(bf16[2,128,256]{2,1,0:T(8,128)(2,1)S(1)} %get-tuple-element.26), channel_id=1, source_target_pairs={{0,4},{4,0},{8,12},{12,8},{16,20},{20,16},{24,28},{28,24},{1,5},{5... | collective-permute-start | bytes 393224 | tf_op jit(solution)/shard_map/ppermute | solution.py:25
  9.3 6.3 %collective-permute-start.2 = (bf16[2,128,256]{2,1,0:T(8,128)(2,1)S(1)}, bf16[2,128,256]{2,1,0:T(8,128)(2,1)S(1)}, u32[]{:S(2)}, u32[]{:S(2)}) collective-permute-start(bf16[2,128,256]{2,1,0:T(8,128)(2,1)S(1)} %get-tuple-element.33), channel_id=1, source_target_pairs={{0,4},{4,0},{8,12},{12,8},{16,20},{20,16},{24,28},{28,24},{1,5},{5... | collective-permute-start | bytes 393224 | tf_op jit(solution)/shard_map/ppermute | solution.py:25
  10.5 6.7 %collective-permute-start.1 = (bf16[2,128,256]{2,1,0:T(8,128)(2,1)S(1)}, bf16[2,128,256]{2,1,0:T(8,128)(2,1)S(1)}, u32[]{:S(2)}, u32[]{:S(2)}) collective-permute-start(bf16[2,128,256]{2,1,0:T(8,128)(2,1)S(1)} %get-tuple-element.32), channel_id=1, source_target_pairs={{0,8},{4,12},{8,0},{12,4},{16,24},{20,28},{24,16},{28,20},{1,9},{5... | collective-permute-start | bytes 393224 | tf_op jit(solution)/shard_map/ppermute | solution.py:25
  12.1 7.4 %collective-permute-start.4 = (bf16[2,128,256]{2,1,0:T(8,128)(2,1)S(1)}, bf16[2,128,256]{2,1,0:T(8,128)(2,1)S(1)}, u32[]{:S(2)}, u32[]{:S(2)}) collective-permute-start(bf16[2,128,256]{2,1,0:T(8,128)(2,1)S(1)} %get-tuple-element.37), channel_id=1, source_target_pairs={{0,4},{4,0},{8,12},{12,8},{16,20},{20,16},{24,28},{28,24},{1,5},{5... | collective-permute-start | bytes 393224 | tf_op jit(solution)/shard_map/ppermute | solution.py:25
  15.7 5.3 %collective-permute-start.5 = (bf16[2,128,256]{2,1,0:T(8,128)(2,1)S(1)}, bf16[2,128,256]{2,1,0:T(8,128)(2,1)S(1)}, u32[]{:S(2)}, u32[]{:S(2)}) collective-permute-start(bf16[2,128,256]{2,1,0:T(8,128)(2,1)S(1)} %get-tuple-element.38), channel_id=1, source_target_pairs={{0,8},{4,12},{8,0},{12,4},{16,24},{20,28},{24,16},{28,20},{1,9},{5... | collective-permute-start | bytes 393224 | tf_op jit(solution)/shard_map/ppermute | solution.py:25
  17.2 7.5 %collective-permute-start.3 = (bf16[2,128,256]{2,1,0:T(8,128)(2,1)S(1)}, bf16[2,128,256]{2,1,0:T(8,128)(2,1)S(1)}, u32[]{:S(2)}, u32[]{:S(2)}) collective-permute-start(bf16[2,128,256]{2,1,0:T(8,128)(2,1)S(1)} %get-tuple-element.36), channel_id=1, source_target_pairs={{0,24},{4,28},{8,16},{12,20},{16,8},{20,12},{24,0},{28,4},{1,25},{... | collective-permute-start | bytes 393224 | tf_op jit(solution)/shard_map/ppermute | solution.py:25
  26.1 2.0 %collective-permute-start.6 = (bf16[2,4,128,256]{3,2,1,0:T(8,128)(2,1)S(1)}, bf16[2,4,128,256]{3,2,1,0:T(8,128)(2,1)S(1)}, u32[]{:S(2)}, u32[]{:S(2)}) collective-permute-start(bf16[2,4,128,256]{3,2,1,0:T(8,128)(2,1)S(1)} %get-tuple-element.40), channel_id=1, source_target_pairs={{0,1},{1,0},{2,3},{3,2},{4,5},{5,4},{6,7},{7,6},{8,9},{9,8},{10,11... | collective-permute-start | bytes 1572872 | tf_op jit(solution)/shard_map/ppermute | solution.py:25
  28.2 8.6 %collective-permute-start.7 = (bf16[1,4,128,256]{3,2,1,0:T(8,128)(2,1)S(1)}, bf16[1,4,128,256]{3,2,1,0:T(8,128)(2,1)S(1)}, u32[]{:S(2)}, u32[]{:S(2)}) collective-permute-start(bf16[1,4,128,256]{3,2,1,0:T(8,128)(2,1)S(1)} %fusion.2), channel_id=1, source_target_pairs={{0,2},{1,3},{2,0},{3,1},{4,6},{5,7},{6,4},{7,5},{8,10},{9,11},{10,... | collective-permute-start | bytes 786440 | tf_op jit(solution)/shard_map/ppermute | solution.py:25

commit v3 on v2

v3 whole, which is shorter than its diff:
```python
import functools

import jax
import jax.numpy as jnp
from jax import lax
from jax.experimental import pallas as pl
from jax.experimental.pallas import tpu as pltpu
from jax.sharding import PartitionSpec as P

CI = 2
SEP = 2
LARGE, SMALL = 24, 12
CHUNKS = 4
BITS = 10
VMEM_LIMIT = 8 << 20

F32 = jnp.float32
BF16 = jnp.bfloat16
VMEM = pl.BlockSpec(memory_space=pltpu.VMEM)
SMEM = pl.BlockSpec(memory_space=pltpu.SMEM)
ANY = pl.BlockSpec(memory_space=pl.ANY)
ALL, TOP, REST, FAR, NEAR, SIZES, PLAN_ROWS = 0, 1, 2, 3, 4, 5, 8


def swap(x, axis, bits):
    return lax.ppermute(x, axis, [(i, i ^ bits) for i in range(lax.axis_size(axis))])


def over_list(plan_ref, which, begin, end, one):
    mask = (1 << BITS) - 1

    def body(size):
        def group(j, base):
            for u in range(size):
                at = base + u
                entry = plan_ref[which, jnp.minimum(at, end - 1)]
                one(entry & mask, (entry >> BITS) & mask, entry >> (2 * BITS), at < end)
            return base + size

        return group

    base = lax.fori_loop(0, (end - begin + LARGE - SMALL - 1) // LARGE, body(LARGE), begin)
    lax.fori_loop(0, (end - base + SMALL - 1) // SMALL, body(SMALL), base)


def project(which, begin, end, low, plan_ref, x_ref, rhs_ref, acc_ref):
    block = x_ref.shape[1]
    trash = acc_ref.shape[0] - 1

    def one(k, row, col, used):
        at = pl.multiple_of(row * block, block)
        acc_ref[jnp.where(used, col - low, trash)] += lax.dot_general(
            x_ref[k], rhs_ref[pl.ds(at, block), :], (((0,), (0,)), ((), ())), preferred_element_type=F32
        )

    over_list(plan_ref, which, begin, end, one)


def image(which, begin, end, low, per, flip, plan_ref, x_ref, coarse_ref, acc_ref):
    trash = acc_ref.shape[0] - 1

    def one(k, row, col, used):
        at = ((row // per) ^ flip) * per + row % per
        acc_ref[jnp.where(used, at, trash)] += jnp.dot(x_ref[k], coarse_ref[col - low], preferred_element_type=F32)

    over_list(plan_ref, which, begin, end, one)


def list_slots(plan_ref, found, low, high, list_len):
    def scan(j, found):
        for u in range(8):
            entry = plan_ref[ALL, j * 8 + u]
            plan_ref[REST, found] = entry
            col = entry >> (2 * BITS)
            found += ((col >= low) & (col < high)).astype(jnp.int32)
        return found

    return lax.fori_loop(0, list_len // 8, scan, found)


def first_kernel(low, high, x_hbm, rhs_hbm, row_hbm, col_hbm, count_hbm, x_ref, rhs_ref, part_ref, half_ref, plan_ref,
                 row_ref, col_ref, count_ref, acc_ref, id_sem, big_sem):
    list_len = x_ref.shape[0]
    chunk = list_len // CHUNKS
    ids = [
        pltpu.make_async_copy(row_hbm, row_ref, id_sem.at[0]),
        pltpu.make_async_copy(col_hbm, col_ref, id_sem.at[1]),
        pltpu.make_async_copy(count_hbm, count_ref, id_sem.at[2]),
    ]
    big = [pltpu.make_async_copy(rhs_hbm, rhs_ref, big_sem.at[CHUNKS])]
    for i in range(CHUNKS):
        at = pl.ds(i * chunk, chunk)
        big.append(pltpu.make_async_copy(x_hbm.at[at], x_ref.at[at], big_sem.at[i]))
    for copy in ids + big:
        copy.start()
    acc_ref[...] = jnp.zeros_like(acc_ref)
    for copy in ids:
        copy.wait()
    count = count_ref[0]

    def scan(j, carry):
        found, second = carry
        for u in range(8):
            k = j * 8 + u
            col = jnp.where(k < count, col_ref[k], high)
            entry = k + (row_ref[k] << BITS) + (col << (2 * BITS))
            plan_ref[ALL, k] = entry
            plan_ref[TOP, found] = entry
            plan_ref[REST, second] = entry
            found += ((col >= low) & (col < high)).astype(jnp.int32)
            second += ((col >= low - SEP) & (col < low)).astype(jnp.int32)
        return found, second

    found, second = lax.fori_loop(0, list_len // 8, scan, (jnp.int32(0), jnp.int32(0)))
    plan_ref[SIZES, TOP] = found
    plan_ref[SIZES, REST] = second
    for copy in big:
        copy.wait()
    project(TOP, jnp.int32(0), found, low, plan_ref, x_ref, rhs_ref, acc_ref)
    for c in range(high - low):
        part_ref[c] = acc_ref[c]
        half_ref[c] = acc_ref[c].astype(BF16)


def part_kernel(low, high, second, old_plan_ref, x_ref, rhs_ref, _, plan_ref, *refs):
    outs, acc_ref = refs[:-1], refs[-1]
    acc_ref[...] = jnp.zeros_like(acc_ref)
    begin, end = jnp.int32(0), plan_ref[SIZES, REST]
    if not second:
        begin, end = end, list_slots(plan_ref, end, low, high, x_ref.shape[0])
        plan_ref[SIZES, REST] = end
    project(REST, begin, end, low, plan_ref, x_ref, rhs_ref, acc_ref)
    for n in range(len(outs) // 2):
        part_ref, half_ref = outs[2 * n : 2 * n + 2]
        for c in range(SEP):
            part_ref[c] = acc_ref[n * SEP + c]
            half_ref[c] = acc_ref[n * SEP + c].astype(BF16)


def add_kernel(own_ref, got_ref, *refs):
    sum_ref, half_ref = refs[-2:]
    total = own_ref[...] + got_ref[...].astype(F32)
    sum_ref[...] = total
    half_ref[...] = total.astype(BF16)


def inner_kernel(per, old_plan_ref, x_ref, rhs_ref, *refs):
    acc_ref, plan_ref, part_ref, coarse_ref = refs[-4:]
    part_ref[...] = jnp.zeros_like(part_ref)
    acc_ref[...] = jnp.zeros_like(acc_ref)
    me = lax.axis_index("col")
    half = (acc_ref.shape[0] - 1) // per // 2

    def scan(j, found):
        far, near = found
        entry = plan_ref[TOP, j]
        plan_ref[FAR, far] = entry
        plan_ref[NEAR, near] = entry
        is_far = (((((entry >> BITS) & ((1 << BITS) - 1)) // per) ^ me) >= half).astype(jnp.int32)
        return far + is_far, near + 1 - is_far

    far, near = lax.fori_loop(0, plan_ref[SIZES, TOP], scan, (jnp.int32(0), jnp.int32(0)))
    plan_ref[SIZES, FAR] = far
    plan_ref[SIZES, NEAR] = near
    begin = plan_ref[SIZES, REST]
    end = list_slots(plan_ref, begin, 0, CI, x_ref.shape[0])
    project(REST, begin, end, 0, plan_ref, x_ref, rhs_ref, part_ref)
    coarse_ref[...] = part_ref[:CI].astype(BF16)
    image(REST, begin, end, 0, per, me, plan_ref, x_ref, coarse_ref, acc_ref)


def mid_kernel(per, plan_ref, x_ref, *refs):
    sums, (old_ref, acc_ref, coarse_ref) = refs[:-3], refs[-3:]
    for n in range(len(sums) // 2):
        own_ref, got_ref = sums[2 * n : 2 * n + 2]
        coarse_ref[n * SEP : (n + 1) * SEP] = (own_ref[...] + got_ref[...].astype(F32)).astype(BF16)
    image(REST, jnp.int32(0), plan_ref[SIZES, REST], CI, per, lax.axis_index("col"), plan_ref, x_ref, coarse_ref, acc_ref)


def split(half, per, acc_ref, keep_ref, send_ref):
    for g in range(keep_ref.shape[0]):
        for b in range(per):
            send_ref[g, b] = acc_ref[half + (2 * g + 1) * per + b].astype(BF16)
            keep_ref[g, b] = acc_ref[half + 2 * g * per + b]


def far_kernel(low, per, plan_ref, x_ref, own_ref, got_ref, old_ref, acc_ref, coarse_ref, keep_ref, send_ref):
    coarse_ref[...] = (own_ref[...] + got_ref[...].astype(F32)).astype(BF16)
    image(FAR, jnp.int32(0), plan_ref[SIZES, FAR], low, per, lax.axis_index("col"), plan_ref, x_ref, coarse_ref, acc_ref)
    split((acc_ref.shape[0] - 1) // 2, per, acc_ref, keep_ref, send_ref)


def near_kernel(low, per, plan_ref, x_ref, coarse_ref, old_ref, acc_ref, keep_ref, send_ref):
    image(NEAR, jnp.int32(0), plan_ref[SIZES, NEAR], low, per, lax.axis_index("col"), plan_ref, x_ref, coarse_ref, acc_ref)
    split(0, per, acc_ref, keep_ref, send_ref)


def body(right_side, x_blocks, row_ids, col_ids, counts):
    blocks, rows, cols, count = x_blocks[0, 0], row_ids[0, 0], col_ids[0, 0], counts[0]
    list_len, block, _ = blocks.shape
    columns = right_side.shape[1]
    row_blocks = right_side.shape[0] // block
    levels = lax.axis_size("leaf").bit_length() - 1
    n_col = lax.axis_size("col")
    per = row_blocks // n_col
    slots = CI + levels * SEP
    low = slots - SEP
    params = pltpu.CompilerParams(vmem_limit_bytes=VMEM_LIMIT)
    free = pl.CostEstimate(flops=0, bytes_accessed=0, transcendentals=0)

    def tiles(n, dtype):
        return pltpu.VMEM((n, block, columns), dtype)

    def in_vmem(*arrays):
        return [pltpu.with_memory_space_constraint(a, pltpu.VMEM) for a in arrays]

    def in_hbm(*arrays):
        return [pltpu.with_memory_space_constraint(a, pltpu.HBM) for a in arrays]

    plan_shape = (PLAN_ROWS, (list_len + 128) // 128 * 128)
    plan_out = pltpu.SMEM(plan_shape, jnp.int32)
    pair = (tiles(SEP, F32), tiles(SEP, BF16))
    sem = pltpu.SemaphoreType.DMA

    x_vmem, rhs_vmem, part, half, plan = pl.pallas_call(
        functools.partial(first_kernel, low, slots),
        out_shape=(pltpu.VMEM(blocks.shape, BF16), pltpu.VMEM(right_side.shape, BF16), *pair, plan_out),
        in_specs=[ANY] * 5,
        out_specs=(*(VMEM,) * 4, SMEM),
        scratch_shapes=[
            pltpu.SMEM((list_len,), jnp.int32),
            pltpu.SMEM((list_len,), jnp.int32),
            pltpu.SMEM((1,), jnp.int32),
            tiles(SEP + 1, F32),
            sem((3,)),
            sem((CHUNKS + 1,)),
        ],
        compiler_params=params,
        cost_estimate=free,
    )(*in_hbm(blocks, right_side, rows, cols), count)
    own, sent, got = {levels: part}, {levels: half}, {}

    def exchange(level, step):
        bits = (2 << step) - 2 if step > 1 else 1 << step
        got[level] = swap(sent[level], "leaf", bits)

    def add(level, *alive):
        own[level], sent[level] = pl.pallas_call(
            add_kernel,
            out_shape=pair,
            in_specs=[VMEM] * (2 + len(alive)),
            out_specs=(VMEM,) * 2,
            compiler_params=params,
            cost_estimate=free,
        )(*in_vmem(own[level], got[level], *alive))

    def parts_of(plan, low, high, second, after):
        pairs = pair * ((high - low) // SEP)
        return pl.pallas_call(
            functools.partial(part_kernel, low, high, second),
            out_shape=(plan_out, *pairs),
            in_specs=[SMEM, VMEM, VMEM, VMEM],
            out_specs=(SMEM, *(VMEM,) * len(pairs)),
            scratch_shapes=[tiles(high - low + 1, F32)],
            input_output_aliases={0: 0},
            compiler_params=params,
            cost_estimate=free,
        )(plan, *in_vmem(x_vmem, rhs_vmem, after))

    plan, own[levels - 1], sent[levels - 1] = parts_of(plan, low - SEP, low, True, own[levels])
    for step in range(levels):
        for level in range(levels, step, -1):
            exchange(level, step if level == levels else level - 1 - step)
            if level > step + 1:
                add(level, x_vmem, rhs_vmem, *[array for n, array in own.items() if n != level])
            if (level, step) == (levels, 0):
                plan, *others = parts_of(plan, CI, low - SEP, False, sent[levels])
                for n in range(levels - 2):
                    own[n + 1], sent[n + 1] = others[2 * n : 2 * n + 2]

    terms, plan = pl.pallas_call(
        functools.partial(inner_kernel, per),
        out_shape=(tiles(row_blocks + 1, F32), plan_out),
        in_specs=[SMEM] + [VMEM] * (3 + len(own)),
        out_specs=(VMEM, SMEM),
        scratch_shapes=[tiles(CI + 1, F32), tiles(CI, BF16)],
        input_output_aliases={0: 1},
        compiler_params=params,
        cost_estimate=free,
    )(plan, *in_vmem(x_vmem, rhs_vmem, sent[levels], *own.values()))

    sums = [array for level in range(1, levels) for array in (own[level], got[level])]
    terms = pl.pallas_call(
        functools.partial(mid_kernel, per),
        out_shape=tiles(row_blocks + 1, F32),
        in_specs=[SMEM] + [VMEM] * (2 + len(sums)),
        out_specs=VMEM,
        scratch_shapes=[tiles(low - CI, BF16)],
        input_output_aliases={2 + len(sums): 0},
        compiler_params=params,
        cost_estimate=free,
    )(plan, *in_vmem(x_vmem, *sums, terms))

    part_shape = (n_col // 4, per, block, columns)
    parts = (pltpu.VMEM(part_shape, F32), pltpu.VMEM(part_shape, BF16))
    terms, coarse, far, far_send = pl.pallas_call(
        functools.partial(far_kernel, low, per),
        out_shape=(tiles(row_blocks + 1, F32), tiles(SEP, BF16), *parts),
        in_specs=[SMEM] + [VMEM] * 4,
        out_specs=(VMEM,) * 4,
        input_output_aliases={4: 0},
        compiler_params=params,
        cost_estimate=free,
    )(plan, *in_vmem(x_vmem, own[levels], got[levels], terms))
    _, near, near_send = pl.pallas_call(
        functools.partial(near_kernel, low, per),
        out_shape=(tiles(row_blocks + 1, F32), *parts),
        in_specs=[SMEM] + [VMEM] * 3,
        out_specs=(VMEM,) * 3,
        input_output_aliases={3: 0},
        compiler_params=params,
        cost_estimate=free,
    )(plan, *in_vmem(x_vmem, coarse, terms))

    def reduce_low_bits(keep, send):
        bit = 1
        while True:
            keep = keep + swap(send, "col", bit).astype(F32)
            bit *= 2
            if bit == n_col // 2:
                return keep[0]
            pairs = keep.reshape(-1, 2, per, block, columns)
            keep, send = pairs[:, 0], pairs[:, 1].astype(BF16)

    far = reduce_low_bits(far, far_send).astype(BF16)
    total = reduce_low_bits(near, near_send) + swap(far, "col", n_col // 2).astype(F32)
    return total.reshape(per * block, columns).astype(BF16)


def solution(mesh):
    in_specs = (
        P("leaf", None),
        P("leaf", "col", None, None, None),
        P("leaf", "col", None),
        P("leaf", "col", None),
        P("leaf", "col"),
    )
    out_specs = P(("leaf", "col"), None)
    return jax.shard_map(body, mesh=mesh, in_specs=in_specs, out_specs=out_specs, check_vma=False)
```

time: 37.9 us -> 34.2 us (0.902)
  waiting for transfers between devices: 13.9 us -> 8.9 us
  Pallas kernels: 8.98 us -> 10.1 us
  starting transfers between devices: 13 us -> 13.6 us
    ppermute x8 -> x9, waiting for transfers between devices: 13.9 us -> 8.9 us  [swap(): lax.ppermute(x, axis, [(i, i ^ bits) for i in range(lax.axis_size(axis))])]
    pallas_call x3 -> x6, Pallas kernels: 6.71 us -> 8.78 us  [the longest x1 3.28 us: body(): pl.pallas_call(functools.partial(first_kernel, low, slots), out_shape=(pl...]
    pallas_call x1, Pallas kernels: 2.16 us -> 1.24 us  [body(): pl.pallas_call(functools.partial(mid_kernel, per), out_shape=tiles(row_bl...]
    ppermute x8 -> x9, starting transfers between devices: 13 us -> 13.6 us  [swap(): lax.ppermute(x, axis, [(i, i ^ bits) for i in range(lax.axis_size(axis))])]
    convert_element_type x1 -> x2, other arithmetic: 0.78 us -> 0.88 us  [the longest x1 0.8 us: body(): return total.reshape(per * block, columns).astype(BF16)]
  transfers between devices with their start and end apart: 8 -> 9, of which waited for: 6 -> 3; matrix products, arithmetic and copies ran while one was open for 0% -> 0% of each run, Pallas kernels for 12% -> 19%
where the time goes in v3:
time: 34.2 us
  starting transfers between devices  13.6 us (40%)
  Pallas kernels  10.1 us (30%)
  waiting for transfers between devices  8.9 us (26%)
  other arithmetic  0.88 us (3%)
  between operations  0.76 us (2%)
    ppermute x9, starting transfers between devices, swap(): lax.ppermute(x, axis, [(i, i ^ bits) for i in range(lax.axis_size(axis))])  13.6 us
    ppermute x9, waiting for transfers between devices, swap(): lax.ppermute(x, axis, [(i, i ^ bits) for i in range(lax.axis_size(axis))])  8.9 us
    pallas_call x1, Pallas kernels, body(): pl.pallas_call(functools.partial(first_kernel, low, slots), out_shape=(pl...  3.28 us
    pallas_call x1, Pallas kernels, body(): pl.pallas_call(functools.partial(inner_kernel, per), out_shape=(tiles(row...  2.4 us
    pallas_call x2, Pallas kernels, parts_of(): pl.pallas_call(functools.partial(part_kernel, low, high, second), out_sha...  1.93 us
    pallas_call x1, Pallas kernels, body(): pl.pallas_call(functools.partial(mid_kernel, per), out_shape=tiles(row_bl...  1.24 us
    convert_element_type x1, other arithmetic, body(): return total.reshape(per * block, columns).astype(BF16)  0.8 us
  transfers between devices with their start and end apart: 9, of which 3 were waited for; matrix products, arithmetic and copies ran while one was open for 0% of the time, Pallas kernels for 19%

profile of v3, /device:TPU:0, one launch (start us, length us, event | category | flops | bytes accessed | tf_op | source)
XLA Modules:
  0.0 34.2 jit_solution(18054044967944284829)
XLA Ops:
  0.7 3.3 %shard_map.55 = (bf16[96,128,128]{2,1,0:T(8,128)(2,1)S(1)}, bf16[2048,256]{1,0:T(8,128)(2,1)S(1)}, f32[2,128,256]{2,1,0:T(8,128)S(1)}, bf16[2,128,256]{2,1,0:T(8,128)(2,1)S(1)}, s32[8,128]{1,0:T(8,128)S(4)}) custom-call(bf16[96,128,128]{2,1,0:T(8,128)(2,1)} %bitcast.12, bf16[2048,256]{1,0:T(8,128)(2,1)} %rhs_hbm.1, s32[96]{0:T(128)} %bitcast.13, ...), custom_call_target="tpu_custom_call" | custom-call | tf_op jit(solution)/shard_map/pallas_call | solution.py:225
  3.9 2.6 %collective-permute-start = (bf16[2,128,256]{2,1,0:T(8,128)(2,1)S(1)}, bf16[2,128,256]{2,1,0:T(8,128)(2,1)S(1)}, u32[]{:S(2)}, u32[]{:S(2)}) collective-permute-start(bf16[2,128,256]{2,1,0:T(8,128)(2,1)S(1)} %get-tuple-element.35), channel_id=1, source_target_pairs={{0,4},{4,0},{8,12},{12,8},{16,20},{20,16},{24,28},{28,24},{1,5},{5... | collective-permute-start | bytes 393224 | tf_op jit(solution)/shard_map/ppermute | solution.py:26
  6.5 0.7 %shard_map.56 = (s32[8,128]{1,0:T(8,128)S(4)}, f32[2,128,256]{2,1,0:T(8,128)S(1)}, bf16[2,128,256]{2,1,0:T(8,128)(2,1)S(1)}) custom-call(s32[8,128]{1,0:T(8,128)S(4)} %get-tuple-element.30.old_plan_ref, bf16[96,128,128]{2,1,0:T(8,128)(2,1)S(1)} %get-tuple-element.31.x_ref.refs_0_, ...), custom_call_target="tpu_custom_call", output_to_operand_aliasing={{0}: (0, {})} | custom-call | tf_op jit(solution)/shard_map/pallas_call | solution.py:259
  7.2 1.4 %collective-permute-start.2 = (bf16[2,128,256]{2,1,0:T(8,128)(2,1)S(1)}, bf16[2,128,256]{2,1,0:T(8,128)(2,1)S(1)}, u32[]{:S(2)}, u32[]{:S(2)}) collective-permute-start(bf16[2,128,256]{2,1,0:T(8,128)(2,1)S(1)} %get-tuple-element.40), channel_id=1, source_target_pairs={{0,8},{4,12},{8,0},{12,4},{16,24},{20,28},{24,16},{28,20},{1,9},{5... | collective-permute-start | bytes 393224 | tf_op jit(solution)/shard_map/ppermute | solution.py:26
  8.7 1.4 %collective-permute-done.got_ref = bf16[2,128,256]{2,1,0:T(8,128)(2,1)S(1)} collective-permute-done((bf16[2,128,256]{2,1,0:T(8,128)(2,1)S(1)}, bf16[2,128,256]{2,1,0:T(8,128)(2,1)S(1)}, u32[]{:S(2)}, u32[]{:S(2)}) %collective-permute-start) | collective-permute-done | bytes 131104 | tf_op jit(solution)/shard_map/ppermute | solution.py:26
  10.1 2.0 %collective-permute-start.1 = (bf16[2,128,256]{2,1,0:T(8,128)(2,1)S(1)}, bf16[2,128,256]{2,1,0:T(8,128)(2,1)S(1)}, u32[]{:S(2)}, u32[]{:S(2)}) collective-permute-start(bf16[2,128,256]{2,1,0:T(8,128)(2,1)S(1)} %get-tuple-element.37._), channel_id=1, source_target_pairs={{0,8},{4,12},{8,0},{12,4},{16,24},{20,28},{24,16},{28,20},{1,9},{5... | collective-permute-start | bytes 393224 | tf_op jit(solution)/shard_map/ppermute | solution.py:26
  12.1 1.3 %shard_map.58 = (s32[8,128]{1,0:T(8,128)S(4)}, f32[2,128,256]{2,1,0:T(8,128)S(1)}, bf16[2,128,256]{2,1,0:T(8,128)(2,1)S(1)}) custom-call(s32[8,128]{1,0:T(8,128)S(4)} %get-tuple-element.34.old_plan_ref, bf16[96,128,128]{2,1,0:T(8,128)(2,1)S(1)} %get-tuple-element.31.x_ref.refs_0_, ...), custom_call_target="tpu_custom_call", output_to_operand_aliasing={{0}: (0, {})} | custom-call | tf_op jit(solution)/shard_map/pallas_call | solution.py:259
  13.4 1.4 %collective-permute-start.4 = (bf16[2,128,256]{2,1,0:T(8,128)(2,1)S(1)}, bf16[2,128,256]{2,1,0:T(8,128)(2,1)S(1)}, u32[]{:S(2)}, u32[]{:S(2)}) collective-permute-start(bf16[2,128,256]{2,1,0:T(8,128)(2,1)S(1)} %get-tuple-element.46), channel_id=1, source_target_pairs={{0,4},{4,0},{8,12},{12,8},{16,20},{20,16},{24,28},{28,24},{1,5},{5... | collective-permute-start | bytes 393224 | tf_op jit(solution)/shard_map/ppermute | solution.py:26
  14.8 0.0 collective-permute-done.2.got_ref
  14.8 0.7 %collective-permute-start.5 = (bf16[2,128,256]{2,1,0:T(8,128)(2,1)S(1)}, bf16[2,128,256]{2,1,0:T(8,128)(2,1)S(1)}, u32[]{:S(2)}, u32[]{:S(2)}) collective-permute-start(bf16[2,128,256]{2,1,0:T(8,128)(2,1)S(1)} %get-tuple-element.47), channel_id=1, source_target_pairs={{0,4},{4,0},{8,12},{12,8},{16,20},{20,16},{24,28},{28,24},{1,5},{5... | collective-permute-start | bytes 393224 | tf_op jit(solution)/shard_map/ppermute | solution.py:26
  15.6 0.0 collective-permute-done.1.got_ref
  15.6 3.6 %collective-permute-start.3 = (bf16[2,128,256]{2,1,0:T(8,128)(2,1)S(1)}, bf16[2,128,256]{2,1,0:T(8,128)(2,1)S(1)}, u32[]{:S(2)}, u32[]{:S(2)}) collective-permute-start(bf16[2,128,256]{2,1,0:T(8,128)(2,1)S(1)} %get-tuple-element.43.refs_0_), channel_id=1, source_target_pairs={{0,24},{4,28},{8,16},{12,20},{16,8},{20,12},{24,0},{28,4},{1,25},{... | collective-permute-start | bytes 393224 | tf_op jit(solution)/shard_map/ppermute | solution.py:26
  19.2 2.4 %shard_map.61 = (f32[17,128,256]{2,1,0:T(8,128)S(1)}, s32[8,128]{1,0:T(8,128)S(4)}) custom-call(s32[8,128]{1,0:T(8,128)S(4)} %get-tuple-element.38.old_plan_ref, bf16[96,128,128]{2,1,0:T(8,128)(2,1)S(1)} %get-tuple-element.31.x_ref.refs_0_, bf16[2048,256]{1,0:T(8,128)(2,1)S(1)} %get-tuple-element.32.rhs_ref.refs_1_, ...), custom_call_target="tpu_custom_call", output_to_operand_aliasing={{1}: (0, {})} | custom-call | tf_op jit(solution)/shard_map/pallas_call | solution.py:281
  21.6 0.0 collective-permute-done.4.refs_1_
  21.6 0.0 collective-permute-done.5.refs_3_
  21.6 1.2 %shard_map.62.old_ref = f32[17,128,256]{2,1,0:T(8,128)S(1)} custom-call(s32[8,128]{1,0:T(8,128)S(4)} %get-tuple-element.45.plan_ref, bf16[96,128,128]{2,1,0:T(8,128)(2,1)S(1)} %get-tuple-element.31.x_ref.refs_0_, f32[2,128,256]{2,1,0:T(8,128)S(1)} %get-tuple-element.41.refs_3_.refs_0_, ...), custom_call_target="tpu_custom_call", output_to_operand_aliasing={{}: (6, {})} | custom-call | tf_op jit(solution)/shard_map/pallas_call | solution.py:293
  22.8 0.0 collective-permute-done.3.got_ref
  22.9 0.5 %shard_map.63 = (f32[17,128,256]{2,1,0:T(8,128)S(1)}, bf16[2,128,256]{2,1,0:T(8,128)(2,1)S(1)}, f32[1,4,128,256]{3,2,1,0:T(8,128)S(1)}, bf16[1,4,128,256]{3,2,1,0:T(8,128)(2,1)S(1)}) custom-call(s32[8,128]{1,0:T(8,128)S(4)} %get-tuple-element.45.plan_ref, bf16[96,128,128]{2,1,0:T(8,128)(2,1)S(1)} %get-tuple-element.31.x_ref.refs_0_, ...), custom_call_target="tpu_custom_call", output_to_operand_aliasing={{0}: (4, {})} | custom-call | tf_op jit(solution)/shard_map/pallas_call | solution.py:306
  23.3 0.1 collective-permute-start.7
  23.4 0.7 %shard_map.64 = (f32[17,128,256]{2,1,0:T(8,128)S(1)}, f32[1,4,128,256]{3,2,1,0:T(8,128)S(1)}, bf16[1,4,128,256]{3,2,1,0:T(8,128)(2,1)S(1)}) custom-call(s32[8,128]{1,0:T(8,128)S(4)} %get-tuple-element.45.plan_ref, bf16[96,128,128]{2,1,0:T(8,128)(2,1)S(1)} %get-tuple-element.31.x_ref.refs_0_, ...), custom_call_target="tpu_custom_call", output_to_operand_aliasing={{0}: (3, {})} | custom-call | tf_op jit(solution)/shard_map/pallas_call | solution.py:315
  24.1 0.5 %collective-permute-start.6 = (bf16[1,4,128,256]{3,2,1,0:T(8,128)(2,1)S(1)}, bf16[1,4,128,256]{3,2,1,0:T(8,128)(2,1)S(1)}, u32[]{:S(2)}, u32[]{:S(2)}) collective-permute-start(bf16[1,4,128,256]{3,2,1,0:T(8,128)(2,1)S(1)} %get-tuple-element.52), channel_id=1, source_target_pairs={{0,1},{1,0},{2,3},{3,2},{4,5},{5,4},{6,7},{7,6},{8,9},{9,8},{10,11... | collective-permute-start | bytes 786440 | tf_op jit(solution)/shard_map/ppermute | solution.py:26
  24.6 0.3 collective-permute-done.7
  24.9 0.1 fusion.1
  25.0 1.2 %collective-permute-start.8 = (bf16[4,128,256]{2,1,0:T(8,128)(2,1)S(1)}, bf16[4,128,256]{2,1,0:T(8,128)(2,1)S(1)}, u32[]{:S(2)}, u32[]{:S(2)}) collective-permute-start(bf16[4,128,256]{2,1,0:T(8,128)(2,1)S(1)} %fusion.1), channel_id=1, source_target_pairs={{0,2},{1,3},{2,0},{3,1},{4,6},{5,7},{6,4},{7,5},{8,10},{9,11},{10,... | collective-permute-start | bytes 786440 | tf_op jit(solution)/shard_map/ppermute | solution.py:26
  26.2 0.0 collective-permute-done.6
  26.2 7.2 %collective-permute-done.8 = bf16[4,128,256]{2,1,0:T(8,128)(2,1)S(1)} collective-permute-done((bf16[4,128,256]{2,1,0:T(8,128)(2,1)S(1)}, bf16[4,128,256]{2,1,0:T(8,128)(2,1)S(1)}, u32[]{:S(2)}, u32[]{:S(2)}) %collective-permute-start.8) | collective-permute-done | bytes 262176 | tf_op jit(solution)/shard_map/ppermute | solution.py:26
  33.4 0.8 %fusion = bf16[4,128,256]{2,1,0:T(8,128)(2,1)} fusion(bf16[4,128,256]{2,1,0:T(8,128)(2,1)S(1)} %collective-permute-done.8, f32[1,4,128,256]{3,2,1,0:T(8,128)S(1)} %get-tuple-element.51, bf16[1,4,128,256]{3,2,1,0:T(8,128)(2,1)S(1)} %collective-permute-done.6), kind=kLoop, calls=%fused_computation.1 | loop fusion | flops 655360 | bytes 1310720 | tf_op jit(solution)/shard_map/convert_element_type | solution.py:337
  (3 shorter events, 0.1 us)
Async XLA Ops:
  3.9 6.1 %collective-permute-start = (bf16[2,128,256]{2,1,0:T(8,128)(2,1)S(1)}, bf16[2,128,256]{2,1,0:T(8,128)(2,1)S(1)}, u32[]{:S(2)}, u32[]{:S(2)}) collective-permute-start(bf16[2,128,256]{2,1,0:T(8,128)(2,1)S(1)} %get-tuple-element.35), channel_id=1, source_target_pairs={{0,4},{4,0},{8,12},{12,8},{16,20},{20,16},{24,28},{28,24},{1,5},{5... | collective-permute-start | bytes 393224 | tf_op jit(solution)/shard_map/ppermute | solution.py:26
  7.2 7.6 %collective-permute-start.2 = (bf16[2,128,256]{2,1,0:T(8,128)(2,1)S(1)}, bf16[2,128,256]{2,1,0:T(8,128)(2,1)S(1)}, u32[]{:S(2)}, u32[]{:S(2)}) collective-permute-start(bf16[2,128,256]{2,1,0:T(8,128)(2,1)S(1)} %get-tuple-element.40), channel_id=1, source_target_pairs={{0,8},{4,12},{8,0},{12,4},{16,24},{20,28},{24,16},{28,20},{1,9},{5... | collective-permute-start | bytes 393224 | tf_op jit(solution)/shard_map/ppermute | solution.py:26
  10.1 5.5 %collective-permute-start.1 = (bf16[2,128,256]{2,1,0:T(8,128)(2,1)S(1)}, bf16[2,128,256]{2,1,0:T(8,128)(2,1)S(1)}, u32[]{:S(2)}, u32[]{:S(2)}) collective-permute-start(bf16[2,128,256]{2,1,0:T(8,128)(2,1)S(1)} %get-tuple-element.37._), channel_id=1, source_target_pairs={{0,8},{4,12},{8,0},{12,4},{16,24},{20,28},{24,16},{28,20},{1,9},{5... | collective-permute-start | bytes 393224 | tf_op jit(solution)/shard_map/ppermute | solution.py:26
  13.4 8.2 %collective-permute-start.4 = (bf16[2,128,256]{2,1,0:T(8,128)(2,1)S(1)}, bf16[2,128,256]{2,1,0:T(8,128)(2,1)S(1)}, u32[]{:S(2)}, u32[]{:S(2)}) collective-permute-start(bf16[2,128,256]{2,1,0:T(8,128)(2,1)S(1)} %get-tuple-element.46), channel_id=1, source_target_pairs={{0,4},{4,0},{8,12},{12,8},{16,20},{20,16},{24,28},{28,24},{1,5},{5... | collective-permute-start | bytes 393224 | tf_op jit(solution)/shard_map/ppermute | solution.py:26
  14.8 6.8 %collective-permute-start.5 = (bf16[2,128,256]{2,1,0:T(8,128)(2,1)S(1)}, bf16[2,128,256]{2,1,0:T(8,128)(2,1)S(1)}, u32[]{:S(2)}, u32[]{:S(2)}) collective-permute-start(bf16[2,128,256]{2,1,0:T(8,128)(2,1)S(1)} %get-tuple-element.47), channel_id=1, source_target_pairs={{0,4},{4,0},{8,12},{12,8},{16,20},{20,16},{24,28},{28,24},{1,5},{5... | collective-permute-start | bytes 393224 | tf_op jit(solution)/shard_map/ppermute | solution.py:26
  15.6 7.2 %collective-permute-start.3 = (bf16[2,128,256]{2,1,0:T(8,128)(2,1)S(1)}, bf16[2,128,256]{2,1,0:T(8,128)(2,1)S(1)}, u32[]{:S(2)}, u32[]{:S(2)}) collective-permute-start(bf16[2,128,256]{2,1,0:T(8,128)(2,1)S(1)} %get-tuple-element.43.refs_0_), channel_id=1, source_target_pairs={{0,24},{4,28},{8,16},{12,20},{16,8},{20,12},{24,0},{28,4},{1,25},{... | collective-permute-start | bytes 393224 | tf_op jit(solution)/shard_map/ppermute | solution.py:26
  23.3 1.6 %collective-permute-start.7 = (bf16[1,4,128,256]{3,2,1,0:T(8,128)(2,1)S(1)}, bf16[1,4,128,256]{3,2,1,0:T(8,128)(2,1)S(1)}, u32[]{:S(2)}, u32[]{:S(2)}) collective-permute-start(bf16[1,4,128,256]{3,2,1,0:T(8,128)(2,1)S(1)} %get-tuple-element.54), channel_id=1, source_target_pairs={{0,1},{1,0},{2,3},{3,2},{4,5},{5,4},{6,7},{7,6},{8,9},{9,8},{10,11... | collective-permute-start | bytes 786440 | tf_op jit(solution)/shard_map/ppermute | solution.py:26
  24.1 2.1 %collective-permute-start.6 = (bf16[1,4,128,256]{3,2,1,0:T(8,128)(2,1)S(1)}, bf16[1,4,128,256]{3,2,1,0:T(8,128)(2,1)S(1)}, u32[]{:S(2)}, u32[]{:S(2)}) collective-permute-start(bf16[1,4,128,256]{3,2,1,0:T(8,128)(2,1)S(1)} %get-tuple-element.52), channel_id=1, source_target_pairs={{0,1},{1,0},{2,3},{3,2},{4,5},{5,4},{6,7},{7,6},{8,9},{9,8},{10,11... | collective-permute-start | bytes 786440 | tf_op jit(solution)/shard_map/ppermute | solution.py:26
  25.0 8.4 %collective-permute-start.8 = (bf16[4,128,256]{2,1,0:T(8,128)(2,1)S(1)}, bf16[4,128,256]{2,1,0:T(8,128)(2,1)S(1)}, u32[]{:S(2)}, u32[]{:S(2)}) collective-permute-start(bf16[4,128,256]{2,1,0:T(8,128)(2,1)S(1)} %fusion.1), channel_id=1, source_target_pairs={{0,2},{1,3},{2,0},{3,1},{4,6},{5,7},{6,4},{7,5},{8,10},{9,11},{10,... | collective-permute-start | bytes 786440 | tf_op jit(solution)/shard_map/ppermute | solution.py:26

commit v4 on v3

--- a/solution.py
+++ b/solution.py
@@ -127,9 +127,13 @@
     acc_ref[...] = jnp.zeros_like(acc_ref)
     begin, end = jnp.int32(0), plan_ref[SIZES, REST]
     if not second:
-        begin, end = end, list_slots(plan_ref, end, low, high, x_ref.shape[0])
-        plan_ref[SIZES, REST] = end
+        begin = plan_ref[SIZES, ALL] if low == 0 else end
+        end = list_slots(plan_ref, begin, low, high, x_ref.shape[0])
+        plan_ref[SIZES, ALL] = end
     project(REST, begin, end, low, plan_ref, x_ref, rhs_ref, acc_ref)
+    if low == 0:
+        for c in range(CI):
+            outs[0][c] = acc_ref[c].astype(BF16)
     for n in range(len(outs) // 2):
         part_ref, half_ref = outs[2 * n : 2 * n + 2]
         for c in range(SEP):
@@ -144,10 +148,17 @@
     half_ref[...] = total.astype(BF16)
 
 
-def inner_kernel(per, old_plan_ref, x_ref, rhs_ref, *refs):
-    acc_ref, plan_ref, part_ref, coarse_ref = refs[-4:]
-    part_ref[...] = jnp.zeros_like(part_ref)
+def sum_coarse(sums, coarse_ref, at):
+    for n in range(len(sums) // 2):
+        own_ref, got_ref = sums[2 * n : 2 * n + 2]
+        coarse_ref[at + n * SEP : at + (n + 1) * SEP] = (own_ref[...] + got_ref[...].astype(F32)).astype(BF16)
+
+
+def lower_kernel(per, levels, old_plan_ref, x_ref, inner_ref, *refs):
+    acc_ref, plan_ref, coarse_ref = refs[-3:]
     acc_ref[...] = jnp.zeros_like(acc_ref)
+    coarse_ref[:CI] = inner_ref[...]
+    sum_coarse(refs[: 2 * levels], coarse_ref, CI)
     me = lax.axis_index("col")
     half = (acc_ref.shape[0] - 1) // per // 2
 
@@ -162,19 +173,12 @@
     far, near = lax.fori_loop(0, plan_ref[SIZES, TOP], scan, (jnp.int32(0), jnp.int32(0)))
     plan_ref[SIZES, FAR] = far
     plan_ref[SIZES, NEAR] = near
-    begin = plan_ref[SIZES, REST]
-    end = list_slots(plan_ref, begin, 0, CI, x_ref.shape[0])
-    project(REST, begin, end, 0, plan_ref, x_ref, rhs_ref, part_ref)
-    coarse_ref[...] = part_ref[:CI].astype(BF16)
-    image(REST, begin, end, 0, per, me, plan_ref, x_ref, coarse_ref, acc_ref)
-
-
-def mid_kernel(per, plan_ref, x_ref, *refs):
-    sums, (old_ref, acc_ref, coarse_ref) = refs[:-3], refs[-3:]
-    for n in range(len(sums) // 2):
-        own_ref, got_ref = sums[2 * n : 2 * n + 2]
-        coarse_ref[n * SEP : (n + 1) * SEP] = (own_ref[...] + got_ref[...].astype(F32)).astype(BF16)
-    image(REST, jnp.int32(0), plan_ref[SIZES, REST], CI, per, lax.axis_index("col"), plan_ref, x_ref, coarse_ref, acc_ref)
+    image(REST, plan_ref[SIZES, REST], plan_ref[SIZES, ALL], 0, per, me, plan_ref, x_ref, coarse_ref, acc_ref)
+
+
+def mid_kernel(per, low, plan_ref, x_ref, own_ref, got_ref, old_ref, acc_ref, coarse_ref):
+    sum_coarse((own_ref, got_ref), coarse_ref, 0)
+    image(REST, jnp.int32(0), plan_ref[SIZES, REST], low, per, lax.axis_index("col"), plan_ref, x_ref, coarse_ref, acc_ref)
 
 
 def split(half, per, acc_ref, keep_ref, send_ref):
@@ -255,7 +259,7 @@
         )(*in_vmem(own[level], got[level], *alive))
 
     def parts_of(plan, low, high, second, after):
-        pairs = pair * ((high - low) // SEP)
+        pairs = (tiles(CI, BF16),) if low == 0 else pair * ((high - low) // SEP)
         return pl.pallas_call(
             functools.partial(part_kernel, low, high, second),
             out_shape=(plan_out, *pairs),
@@ -268,38 +272,42 @@
         )(plan, *in_vmem(x_vmem, rhs_vmem, after))
 
     plan, own[levels - 1], sent[levels - 1] = parts_of(plan, low - SEP, low, True, own[levels])
+    plan, *others = parts_of(plan, CI, low - SEP, False, own[levels])
+    for n in range(levels - 2):
+        own[n + 1], sent[n + 1] = others[2 * n : 2 * n + 2]
+    inner = []
     for step in range(levels):
         for level in range(levels, step, -1):
             exchange(level, step if level == levels else level - 1 - step)
             if level > step + 1:
-                add(level, x_vmem, rhs_vmem, *[array for n, array in own.items() if n != level])
+                add(level, x_vmem, rhs_vmem, *inner, *[array for n, array in own.items() if n != level])
             if (level, step) == (levels, 0):
-                plan, *others = parts_of(plan, CI, low - SEP, False, sent[levels])
-                for n in range(levels - 2):
-                    own[n + 1], sent[n + 1] = others[2 * n : 2 * n + 2]
-
+                plan, *inner = parts_of(plan, 0, CI, False, sent[levels])
+
+    sums = [array for level in range(1, levels - 1) for array in (own[level], got[level])]
+    alive = [sent[levels], own[levels], own[levels - 1]]
     terms, plan = pl.pallas_call(
-        functools.partial(inner_kernel, per),
+        functools.partial(lower_kernel, per, levels - 2),
         out_shape=(tiles(row_blocks + 1, F32), plan_out),
-        in_specs=[SMEM] + [VMEM] * (3 + len(own)),
+        in_specs=[SMEM] + [VMEM] * (2 + len(sums) + len(alive)),
         out_specs=(VMEM, SMEM),
-        scratch_shapes=[tiles(CI + 1, F32), tiles(CI, BF16)],
+        scratch_shapes=[tiles(low - SEP, BF16)],
         input_output_aliases={0: 1},
         compiler_params=params,
         cost_estimate=free,
-    )(plan, *in_vmem(x_vmem, rhs_vmem, sent[levels], *own.values()))
-
-    sums = [array for level in range(1, levels) for array in (own[level], got[level])]
+    )(plan, *in_vmem(x_vmem, *inner, *sums, *alive))
+
+    second = levels - 1
     terms = pl.pallas_call(
-        functools.partial(mid_kernel, per),
+        functools.partial(mid_kernel, per, low - SEP),
         out_shape=tiles(row_blocks + 1, F32),
-        in_specs=[SMEM] + [VMEM] * (2 + len(sums)),
+        in_specs=[SMEM] + [VMEM] * 4,
         out_specs=VMEM,
-        scratch_shapes=[tiles(low - CI, BF16)],
-        input_output_aliases={2 + len(sums): 0},
-        compiler_params=params,
-        cost_estimate=free,
-    )(plan, *in_vmem(x_vmem, *sums, terms))
+        scratch_shapes=[tiles(SEP, BF16)],
+        input_output_aliases={4: 0},
+        compiler_params=params,
+        cost_estimate=free,
+    )(plan, *in_vmem(x_vmem, own[second], got[second], terms))
 
     part_shape = (n_col // 4, per, block, columns)
     parts = (pltpu.VMEM(part_shape, F32), pltpu.VMEM(part_shape, BF16))

time: 34.2 us -> 34.1 us (level)
  starting transfers between devices: 13.6 us -> 14.8 us
  waiting for transfers between devices: 8.9 us -> 7.96 us
  Pallas kernels: 10.1 us -> 9.4 us
    pallas_call x2, Pallas kernels: 3.63 us -> 2.29 us  [the longest x1 1.66 us: body(): pl.pallas_call(functools.partial(lower_kernel, per, levels - 2), out_shap...]
    pallas_call x2 -> x3, Pallas kernels: 1.93 us -> 3.18 us  [parts_of(): pl.pallas_call(functools.partial(part_kernel, low, high, second), out_sha...]
    ppermute x9, starting transfers between devices: 13.6 us -> 14.8 us  [swap(): lax.ppermute(x, axis, [(i, i ^ bits) for i in range(lax.axis_size(axis))])]
    ppermute x9, waiting for transfers between devices: 8.9 us -> 7.96 us  [swap(): lax.ppermute(x, axis, [(i, i ^ bits) for i in range(lax.axis_size(axis))])]
    pallas_call x1, Pallas kernels: 3.28 us -> 2.87 us  [body(): pl.pallas_call(functools.partial(first_kernel, low, slots), out_shape=(pl...]
  transfers between devices with their start and end apart: 9 -> 9, of which waited for: 3 -> 3; matrix products, arithmetic and copies ran while one was open for 0% -> 0% of each run, Pallas kernels for 19% -> 18%
where the time goes in v4:
time: 34.1 us; the launch traced here: 33.8 us
  starting transfers between devices  14.8 us (43%)
  Pallas kernels  9.4 us (28%)
  waiting for transfers between devices  7.96 us (23%)
  other arithmetic  0.87 us (3%)
  between operations  0.77 us (2%)
    ppermute x9, starting transfers between devices, swap(): lax.ppermute(x, axis, [(i, i ^ bits) for i in range(lax.axis_size(axis))])  14.8 us
    ppermute x9, waiting for transfers between devices, swap(): lax.ppermute(x, axis, [(i, i ^ bits) for i in range(lax.axis_size(axis))])  7.96 us
    pallas_call x3, Pallas kernels, parts_of(): pl.pallas_call(functools.partial(part_kernel, low, high, second), out_sha...  3.18 us
    pallas_call x1, Pallas kernels, body(): pl.pallas_call(functools.partial(first_kernel, low, slots), out_shape=(pl...  2.87 us
    pallas_call x1, Pallas kernels, body(): pl.pallas_call(functools.partial(lower_kernel, per, levels - 2), out_shap...  1.66 us
    convert_element_type x1, other arithmetic, body(): return total.reshape(per * block, columns).astype(BF16)  0.8 us
  transfers between devices with their start and end apart: 9, of which 3 were waited for; matrix products, arithmetic and copies ran while one was open for 0% of the time, Pallas kernels for 18%

profile of v4, /device:TPU:0, one launch (start us, length us, event | category | flops | bytes accessed | tf_op | source)
XLA Modules:
  0.0 33.8 jit_solution(15697599602768282130)
XLA Ops:
  0.7 2.9 %shard_map.55 = (bf16[96,128,128]{2,1,0:T(8,128)(2,1)S(1)}, bf16[2048,256]{1,0:T(8,128)(2,1)S(1)}, f32[2,128,256]{2,1,0:T(8,128)S(1)}, bf16[2,128,256]{2,1,0:T(8,128)(2,1)S(1)}, s32[8,128]{1,0:T(8,128)S(4)}) custom-call(bf16[96,128,128]{2,1,0:T(8,128)(2,1)} %bitcast.12, bf16[2048,256]{1,0:T(8,128)(2,1)} %rhs_hbm.1, s32[96]{0:T(128)} %bitcast.13, ...), custom_call_target="tpu_custom_call" | custom-call | tf_op jit(solution)/shard_map/pallas_call | solution.py:229
  3.5 2.8 %collective-permute-start = (bf16[2,128,256]{2,1,0:T(8,128)(2,1)S(1)}, bf16[2,128,256]{2,1,0:T(8,128)(2,1)S(1)}, u32[]{:S(2)}, u32[]{:S(2)}) collective-permute-start(bf16[2,128,256]{2,1,0:T(8,128)(2,1)S(1)} %get-tuple-element.38), channel_id=1, source_target_pairs={{0,4},{4,0},{8,12},{12,8},{16,20},{20,16},{24,28},{28,24},{1,5},{5... | collective-permute-start | bytes 393224 | tf_op jit(solution)/shard_map/ppermute | solution.py:26
  6.3 0.7 %shard_map.56 = (s32[8,128]{1,0:T(8,128)S(4)}, f32[2,128,256]{2,1,0:T(8,128)S(1)}, bf16[2,128,256]{2,1,0:T(8,128)(2,1)S(1)}) custom-call(s32[8,128]{1,0:T(8,128)S(4)} %get-tuple-element.32.old_plan_ref, bf16[96,128,128]{2,1,0:T(8,128)(2,1)S(1)} %get-tuple-element.33.x_ref.refs_0_, ...), custom_call_target="tpu_custom_call", output_to_operand_aliasing={{0}: (0, {})} | custom-call | tf_op jit(solution)/shard_map/pallas_call | solution.py:263
  7.0 1.9 %collective-permute-start.3 = (bf16[2,128,256]{2,1,0:T(8,128)(2,1)S(1)}, bf16[2,128,256]{2,1,0:T(8,128)(2,1)S(1)}, u32[]{:S(2)}, u32[]{:S(2)}) collective-permute-start(bf16[2,128,256]{2,1,0:T(8,128)(2,1)S(1)} %get-tuple-element.46), channel_id=1, source_target_pairs={{0,8},{4,12},{8,0},{12,4},{16,24},{20,28},{24,16},{28,20},{1,9},{5... | collective-permute-start | bytes 393224 | tf_op jit(solution)/shard_map/ppermute | solution.py:26
  8.9 1.3 %shard_map.57 = (s32[8,128]{1,0:T(8,128)S(4)}, f32[2,128,256]{2,1,0:T(8,128)S(1)}, bf16[2,128,256]{2,1,0:T(8,128)(2,1)S(1)}) custom-call(s32[8,128]{1,0:T(8,128)S(4)} %get-tuple-element.36.old_plan_ref, bf16[96,128,128]{2,1,0:T(8,128)(2,1)S(1)} %get-tuple-element.33.x_ref.refs_0_, ...), custom_call_target="tpu_custom_call", output_to_operand_aliasing={{0}: (0, {})} | custom-call | tf_op jit(solution)/shard_map/pallas_call | solution.py:263
  10.1 0.0 collective-permute-done.got_ref
  10.2 1.8 %collective-permute-start.2 = (bf16[2,128,256]{2,1,0:T(8,128)(2,1)S(1)}, bf16[2,128,256]{2,1,0:T(8,128)(2,1)S(1)}, u32[]{:S(2)}, u32[]{:S(2)}) collective-permute-start(bf16[2,128,256]{2,1,0:T(8,128)(2,1)S(1)} %get-tuple-element.41._), channel_id=1, source_target_pairs={{0,8},{4,12},{8,0},{12,4},{16,24},{20,28},{24,16},{28,20},{1,9},{5... | collective-permute-start | bytes 393224 | tf_op jit(solution)/shard_map/ppermute | solution.py:26
  12.0 1.5 %collective-permute-start.1 = (bf16[2,128,256]{2,1,0:T(8,128)(2,1)S(1)}, bf16[2,128,256]{2,1,0:T(8,128)(2,1)S(1)}, u32[]{:S(2)}, u32[]{:S(2)}) collective-permute-start(bf16[2,128,256]{2,1,0:T(8,128)(2,1)S(1)} %get-tuple-element.44), channel_id=1, source_target_pairs={{0,4},{4,0},{8,12},{12,8},{16,20},{20,16},{24,28},{28,24},{1,5},{5... | collective-permute-start | bytes 393224 | tf_op jit(solution)/shard_map/ppermute | solution.py:26
  13.5 1.2 %shard_map.59 = (s32[8,128]{1,0:T(8,128)S(4)}, bf16[2,128,256]{2,1,0:T(8,128)(2,1)S(1)}) custom-call(s32[8,128]{1,0:T(8,128)S(4)} %get-tuple-element.37.old_plan_ref, bf16[96,128,128]{2,1,0:T(8,128)(2,1)S(1)} %get-tuple-element.33.x_ref.refs_0_, bf16[2048,256]{1,0:T(8,128)(2,1)S(1)} %get-tuple-element.34.rhs_ref.refs_1_, ...), custom_call_target="tpu_custom_call", output_to_operand_aliasing={{0}: (0, {})} | custom-call | tf_op jit(solution)/shard_map/pallas_call | solution.py:263
  14.7 0.0 collective-permute-done.3.got_ref
  14.8 0.6 %collective-permute-start.5 = (bf16[2,128,256]{2,1,0:T(8,128)(2,1)S(1)}, bf16[2,128,256]{2,1,0:T(8,128)(2,1)S(1)}, u32[]{:S(2)}, u32[]{:S(2)}) collective-permute-start(bf16[2,128,256]{2,1,0:T(8,128)(2,1)S(1)} %get-tuple-element.51), channel_id=1, source_target_pairs={{0,4},{4,0},{8,12},{12,8},{16,20},{20,16},{24,28},{28,24},{1,5},{5... | collective-permute-start | bytes 393224 | tf_op jit(solution)/shard_map/ppermute | solution.py:26
  15.4 0.0 collective-permute-done.2.got_ref
  15.4 3.8 %collective-permute-start.4 = (bf16[2,128,256]{2,1,0:T(8,128)(2,1)S(1)}, bf16[2,128,256]{2,1,0:T(8,128)(2,1)S(1)}, u32[]{:S(2)}, u32[]{:S(2)}) collective-permute-start(bf16[2,128,256]{2,1,0:T(8,128)(2,1)S(1)} %get-tuple-element.48.refs_2_), channel_id=1, source_target_pairs={{0,24},{4,28},{8,16},{12,20},{16,8},{20,12},{24,0},{28,4},{1,25},{... | collective-permute-start | bytes 393224 | tf_op jit(solution)/shard_map/ppermute | solution.py:26
  19.2 0.0 collective-permute-done.1.refs_1_
  19.2 1.7 %shard_map.62 = (f32[17,128,256]{2,1,0:T(8,128)S(1)}, s32[8,128]{1,0:T(8,128)S(4)}) custom-call(s32[8,128]{1,0:T(8,128)S(4)} %get-tuple-element.42.old_plan_ref, bf16[96,128,128]{2,1,0:T(8,128)(2,1)S(1)} %get-tuple-element.33.x_ref.refs_0_, bf16[2,128,256]{2,1,0:T(8,128)(2,1)S(1)} %get-tuple-element.43.refs_2_.inner_ref, ...), custom_call_target="tpu_custom_call", output_to_operand_aliasing={{1}: (0, {})} | custom-call | tf_op jit(solution)/shard_map/pallas_call | solution.py:289
  20.9 0.0 collective-permute-done.5.got_ref
  20.9 0.6 %shard_map.63.old_ref = f32[17,128,256]{2,1,0:T(8,128)S(1)} custom-call(s32[8,128]{1,0:T(8,128)S(4)} %get-tuple-element.50.plan_ref, bf16[96,128,128]{2,1,0:T(8,128)(2,1)S(1)} %get-tuple-element.33.x_ref.refs_0_, f32[2,128,256]{2,1,0:T(8,128)S(1)} %get-tuple-element.47.refs_3_.refs_4_.own_ref, ...), custom_call_target="tpu_custom_call", output_to_operand_aliasing={{}: (4, {})} | custom-call | tf_op jit(solution)/shard_map/pallas_call | solution.py:301
  21.5 0.8 %collective-permute-done.4.got_ref = bf16[2,128,256]{2,1,0:T(8,128)(2,1)S(1)} collective-permute-done((bf16[2,128,256]{2,1,0:T(8,128)(2,1)S(1)}, bf16[2,128,256]{2,1,0:T(8,128)(2,1)S(1)}, u32[]{:S(2)}, u32[]{:S(2)}) %collective-permute-start.4) | collective-permute-done | bytes 131104 | tf_op jit(solution)/shard_map/ppermute | solution.py:26
  22.3 0.5 %shard_map.64 = (f32[17,128,256]{2,1,0:T(8,128)S(1)}, bf16[2,128,256]{2,1,0:T(8,128)(2,1)S(1)}, f32[1,4,128,256]{3,2,1,0:T(8,128)S(1)}, bf16[1,4,128,256]{3,2,1,0:T(8,128)(2,1)S(1)}) custom-call(s32[8,128]{1,0:T(8,128)S(4)} %get-tuple-element.50.plan_ref, bf16[96,128,128]{2,1,0:T(8,128)(2,1)S(1)} %get-tuple-element.33.x_ref.refs_0_, ...), custom_call_target="tpu_custom_call", output_to_operand_aliasing={{0}: (4, {})} | custom-call | tf_op jit(solution)/shard_map/pallas_call | solution.py:314
  22.8 0.1 collective-permute-start.7
  22.9 0.5 %shard_map.65 = (f32[17,128,256]{2,1,0:T(8,128)S(1)}, f32[1,4,128,256]{3,2,1,0:T(8,128)S(1)}, bf16[1,4,128,256]{3,2,1,0:T(8,128)(2,1)S(1)}) custom-call(s32[8,128]{1,0:T(8,128)S(4)} %get-tuple-element.50.plan_ref, bf16[96,128,128]{2,1,0:T(8,128)(2,1)S(1)} %get-tuple-element.33.x_ref.refs_0_, ...), custom_call_target="tpu_custom_call", output_to_operand_aliasing={{0}: (3, {})} | custom-call | tf_op jit(solution)/shard_map/pallas_call | solution.py:323
  23.4 0.5 %collective-permute-start.6 = (bf16[1,4,128,256]{3,2,1,0:T(8,128)(2,1)S(1)}, bf16[1,4,128,256]{3,2,1,0:T(8,128)(2,1)S(1)}, u32[]{:S(2)}, u32[]{:S(2)}) collective-permute-start(bf16[1,4,128,256]{3,2,1,0:T(8,128)(2,1)S(1)} %get-tuple-element.56), channel_id=1, source_target_pairs={{0,1},{1,0},{2,3},{3,2},{4,5},{5,4},{6,7},{7,6},{8,9},{9,8},{10,11... | collective-permute-start | bytes 786440 | tf_op jit(solution)/shard_map/ppermute | solution.py:26
  23.9 0.5 %collective-permute-done.7 = bf16[1,4,128,256]{3,2,1,0:T(8,128)(2,1)S(1)} collective-permute-done((bf16[1,4,128,256]{3,2,1,0:T(8,128)(2,1)S(1)}, bf16[1,4,128,256]{3,2,1,0:T(8,128)(2,1)S(1)}, u32[]{:S(2)}, u32[]{:S(2)}) %collective-permute-start.7) | collective-permute-done | bytes 262176 | tf_op jit(solution)/shard_map/ppermute | solution.py:26
  24.4 0.1 fusion.1
  24.5 1.9 %collective-permute-start.8 = (bf16[4,128,256]{2,1,0:T(8,128)(2,1)S(1)}, bf16[4,128,256]{2,1,0:T(8,128)(2,1)S(1)}, u32[]{:S(2)}, u32[]{:S(2)}) collective-permute-start(bf16[4,128,256]{2,1,0:T(8,128)(2,1)S(1)} %fusion.1), channel_id=1, source_target_pairs={{0,2},{1,3},{2,0},{3,1},{4,6},{5,7},{6,4},{7,5},{8,10},{9,11},{10,... | collective-permute-start | bytes 786440 | tf_op jit(solution)/shard_map/ppermute | solution.py:26
  26.4 0.0 collective-permute-done.6
  26.4 6.6 %collective-permute-done.8 = bf16[4,128,256]{2,1,0:T(8,128)(2,1)S(1)} collective-permute-done((bf16[4,128,256]{2,1,0:T(8,128)(2,1)S(1)}, bf16[4,128,256]{2,1,0:T(8,128)(2,1)S(1)}, u32[]{:S(2)}, u32[]{:S(2)}) %collective-permute-start.8) | collective-permute-done | bytes 262176 | tf_op jit(solution)/shard_map/ppermute | solution.py:26
  33.0 0.8 %fusion = bf16[4,128,256]{2,1,0:T(8,128)(2,1)} fusion(bf16[4,128,256]{2,1,0:T(8,128)(2,1)S(1)} %collective-permute-done.8, f32[1,4,128,256]{3,2,1,0:T(8,128)S(1)} %get-tuple-element.55, bf16[1,4,128,256]{3,2,1,0:T(8,128)(2,1)S(1)} %collective-permute-done.6), kind=kLoop, calls=%fused_computation.1 | loop fusion | flops 655360 | bytes 1310720 | tf_op jit(solution)/shard_map/convert_element_type | solution.py:345
  (3 shorter events, 0.1 us)
Async XLA Ops:
  3.5 6.6 %collective-permute-start = (bf16[2,128,256]{2,1,0:T(8,128)(2,1)S(1)}, bf16[2,128,256]{2,1,0:T(8,128)(2,1)S(1)}, u32[]{:S(2)}, u32[]{:S(2)}) collective-permute-start(bf16[2,128,256]{2,1,0:T(8,128)(2,1)S(1)} %get-tuple-element.38), channel_id=1, source_target_pairs={{0,4},{4,0},{8,12},{12,8},{16,20},{20,16},{24,28},{28,24},{1,5},{5... | collective-permute-start | bytes 393224 | tf_op jit(solution)/shard_map/ppermute | solution.py:26
  7.0 7.7 %collective-permute-start.3 = (bf16[2,128,256]{2,1,0:T(8,128)(2,1)S(1)}, bf16[2,128,256]{2,1,0:T(8,128)(2,1)S(1)}, u32[]{:S(2)}, u32[]{:S(2)}) collective-permute-start(bf16[2,128,256]{2,1,0:T(8,128)(2,1)S(1)} %get-tuple-element.46), channel_id=1, source_target_pairs={{0,8},{4,12},{8,0},{12,4},{16,24},{20,28},{24,16},{28,20},{1,9},{5... | collective-permute-start | bytes 393224 | tf_op jit(solution)/shard_map/ppermute | solution.py:26
  10.2 5.2 %collective-permute-start.2 = (bf16[2,128,256]{2,1,0:T(8,128)(2,1)S(1)}, bf16[2,128,256]{2,1,0:T(8,128)(2,1)S(1)}, u32[]{:S(2)}, u32[]{:S(2)}) collective-permute-start(bf16[2,128,256]{2,1,0:T(8,128)(2,1)S(1)} %get-tuple-element.41._), channel_id=1, source_target_pairs={{0,8},{4,12},{8,0},{12,4},{16,24},{20,28},{24,16},{28,20},{1,9},{5... | collective-permute-start | bytes 393224 | tf_op jit(solution)/shard_map/ppermute | solution.py:26
  12.0 7.2 %collective-permute-start.1 = (bf16[2,128,256]{2,1,0:T(8,128)(2,1)S(1)}, bf16[2,128,256]{2,1,0:T(8,128)(2,1)S(1)}, u32[]{:S(2)}, u32[]{:S(2)}) collective-permute-start(bf16[2,128,256]{2,1,0:T(8,128)(2,1)S(1)} %get-tuple-element.44), channel_id=1, source_target_pairs={{0,4},{4,0},{8,12},{12,8},{16,20},{20,16},{24,28},{28,24},{1,5},{5... | collective-permute-start | bytes 393224 | tf_op jit(solution)/shard_map/ppermute | solution.py:26
  14.8 6.1 %collective-permute-start.5 = (bf16[2,128,256]{2,1,0:T(8,128)(2,1)S(1)}, bf16[2,128,256]{2,1,0:T(8,128)(2,1)S(1)}, u32[]{:S(2)}, u32[]{:S(2)}) collective-permute-start(bf16[2,128,256]{2,1,0:T(8,128)(2,1)S(1)} %get-tuple-element.51), channel_id=1, source_target_pairs={{0,4},{4,0},{8,12},{12,8},{16,20},{20,16},{24,28},{28,24},{1,5},{5... | collective-permute-start | bytes 393224 | tf_op jit(solution)/shard_map/ppermute | solution.py:26
  15.4 6.9 %collective-permute-start.4 = (bf16[2,128,256]{2,1,0:T(8,128)(2,1)S(1)}, bf16[2,128,256]{2,1,0:T(8,128)(2,1)S(1)}, u32[]{:S(2)}, u32[]{:S(2)}) collective-permute-start(bf16[2,128,256]{2,1,0:T(8,128)(2,1)S(1)} %get-tuple-element.48.refs_2_), channel_id=1, source_target_pairs={{0,24},{4,28},{8,16},{12,20},{16,8},{20,12},{24,0},{28,4},{1,25},{... | collective-permute-start | bytes 393224 | tf_op jit(solution)/shard_map/ppermute | solution.py:26
  22.8 1.6 %collective-permute-start.7 = (bf16[1,4,128,256]{3,2,1,0:T(8,128)(2,1)S(1)}, bf16[1,4,128,256]{3,2,1,0:T(8,128)(2,1)S(1)}, u32[]{:S(2)}, u32[]{:S(2)}) collective-permute-start(bf16[1,4,128,256]{3,2,1,0:T(8,128)(2,1)S(1)} %get-tuple-element.58), channel_id=1, source_target_pairs={{0,1},{1,0},{2,3},{3,2},{4,5},{5,4},{6,7},{7,6},{8,9},{9,8},{10,11... | collective-permute-start | bytes 786440 | tf_op jit(solution)/shard_map/ppermute | solution.py:26
  23.4 3.0 %collective-permute-start.6 = (bf16[1,4,128,256]{3,2,1,0:T(8,128)(2,1)S(1)}, bf16[1,4,128,256]{3,2,1,0:T(8,128)(2,1)S(1)}, u32[]{:S(2)}, u32[]{:S(2)}) collective-permute-start(bf16[1,4,128,256]{3,2,1,0:T(8,128)(2,1)S(1)} %get-tuple-element.56), channel_id=1, source_target_pairs={{0,1},{1,0},{2,3},{3,2},{4,5},{5,4},{6,7},{7,6},{8,9},{9,8},{10,11... | collective-permute-start | bytes 786440 | tf_op jit(solution)/shard_map/ppermute | solution.py:26
  24.5 8.5 %collective-permute-start.8 = (bf16[4,128,256]{2,1,0:T(8,128)(2,1)S(1)}, bf16[4,128,256]{2,1,0:T(8,128)(2,1)S(1)}, u32[]{:S(2)}, u32[]{:S(2)}) collective-permute-start(bf16[4,128,256]{2,1,0:T(8,128)(2,1)S(1)} %fusion.1), channel_id=1, source_target_pairs={{0,2},{1,3},{2,0},{3,1},{4,6},{5,7},{6,4},{7,5},{8,10},{9,11},{10,... | collective-permute-start | bytes 786440 | tf_op jit(solution)/shard_map/ppermute | solution.py:26

commit v5 on v4

--- a/solution.py
+++ b/solution.py
@@ -9,7 +9,7 @@
 
 CI = 2
 SEP = 2
-LARGE, SMALL = 24, 12
+LARGE, SMALL = 32, 16
 CHUNKS = 4
 BITS = 10
 VMEM_LIMIT = 8 << 20

time: 34.1 us -> 34.1 us (level)
  waiting for transfers between devices: 7.96 us -> 8.77 us
  starting transfers between devices: 14.8 us -> 14.4 us
    ppermute x9, waiting for transfers between devices: 7.96 us -> 8.77 us  [swap(): lax.ppermute(x, axis, [(i, i ^ bits) for i in range(lax.axis_size(axis))])]
    ppermute x9, starting transfers between devices: 14.8 us -> 14.4 us  [swap(): lax.ppermute(x, axis, [(i, i ^ bits) for i in range(lax.axis_size(axis))])]
where the time goes in v5:
time: 34.1 us; the launch traced here: 34 us
  starting transfers between devices  14.4 us (42%)
  Pallas kernels  9.24 us (27%)
  waiting for transfers between devices  8.77 us (26%)
  other arithmetic  0.87 us (3%)
  between operations  0.77 us (2%)
    ppermute x9, starting transfers between devices, swap(): lax.ppermute(x, axis, [(i, i ^ bits) for i in range(lax.axis_size(axis))])  14.4 us
    ppermute x9, waiting for transfers between devices, swap(): lax.ppermute(x, axis, [(i, i ^ bits) for i in range(lax.axis_size(axis))])  8.77 us
    pallas_call x3, Pallas kernels, parts_of(): pl.pallas_call(functools.partial(part_kernel, low, high, second), out_sha...  3.29 us
    pallas_call x1, Pallas kernels, body(): pl.pallas_call(functools.partial(first_kernel, low, slots), out_shape=(pl...  2.72 us
    pallas_call x1, Pallas kernels, body(): pl.pallas_call(functools.partial(lower_kernel, per, levels - 2), out_shap...  1.55 us
    convert_element_type x1, other arithmetic, body(): return total.reshape(per * block, columns).astype(BF16)  0.8 us
  transfers between devices with their start and end apart: 9, of which 3 were waited for; matrix products, arithmetic and copies ran while one was open for 0% of the time, Pallas kernels for 18%

profile of v5, /device:TPU:0, one launch (start us, length us, event | category | flops | bytes accessed | tf_op | source)
XLA Modules:
  0.0 34.0 jit_solution(16368087725704636280)
XLA Ops:
  0.7 2.7 %shard_map.55 = (bf16[96,128,128]{2,1,0:T(8,128)(2,1)S(1)}, bf16[2048,256]{1,0:T(8,128)(2,1)S(1)}, f32[2,128,256]{2,1,0:T(8,128)S(1)}, bf16[2,128,256]{2,1,0:T(8,128)(2,1)S(1)}, s32[8,128]{1,0:T(8,128)S(4)}) custom-call(bf16[96,128,128]{2,1,0:T(8,128)(2,1)} %bitcast.12, bf16[2048,256]{1,0:T(8,128)(2,1)} %rhs_hbm.1, s32[96]{0:T(128)} %bitcast.13, ...), custom_call_target="tpu_custom_call" | custom-call | tf_op jit(solution)/shard_map/pallas_call | solution.py:229
  3.4 3.0 %collective-permute-start = (bf16[2,128,256]{2,1,0:T(8,128)(2,1)S(1)}, bf16[2,128,256]{2,1,0:T(8,128)(2,1)S(1)}, u32[]{:S(2)}, u32[]{:S(2)}) collective-permute-start(bf16[2,128,256]{2,1,0:T(8,128)(2,1)S(1)} %get-tuple-element.38), channel_id=1, source_target_pairs={{0,4},{4,0},{8,12},{12,8},{16,20},{20,16},{24,28},{28,24},{1,5},{5... | collective-permute-start | bytes 393224 | tf_op jit(solution)/shard_map/ppermute | solution.py:26
  6.4 0.5 %shard_map.56 = (s32[8,128]{1,0:T(8,128)S(4)}, f32[2,128,256]{2,1,0:T(8,128)S(1)}, bf16[2,128,256]{2,1,0:T(8,128)(2,1)S(1)}) custom-call(s32[8,128]{1,0:T(8,128)S(4)} %get-tuple-element.32.old_plan_ref, bf16[96,128,128]{2,1,0:T(8,128)(2,1)S(1)} %get-tuple-element.33.x_ref.refs_0_, ...), custom_call_target="tpu_custom_call", output_to_operand_aliasing={{0}: (0, {})} | custom-call | tf_op jit(solution)/shard_map/pallas_call | solution.py:263
  6.9 1.9 %collective-permute-start.3 = (bf16[2,128,256]{2,1,0:T(8,128)(2,1)S(1)}, bf16[2,128,256]{2,1,0:T(8,128)(2,1)S(1)}, u32[]{:S(2)}, u32[]{:S(2)}) collective-permute-start(bf16[2,128,256]{2,1,0:T(8,128)(2,1)S(1)} %get-tuple-element.46), channel_id=1, source_target_pairs={{0,8},{4,12},{8,0},{12,4},{16,24},{20,28},{24,16},{28,20},{1,9},{5... | collective-permute-start | bytes 393224 | tf_op jit(solution)/shard_map/ppermute | solution.py:26
  8.8 1.4 %shard_map.57 = (s32[8,128]{1,0:T(8,128)S(4)}, f32[2,128,256]{2,1,0:T(8,128)S(1)}, bf16[2,128,256]{2,1,0:T(8,128)(2,1)S(1)}) custom-call(s32[8,128]{1,0:T(8,128)S(4)} %get-tuple-element.36.old_plan_ref, bf16[96,128,128]{2,1,0:T(8,128)(2,1)S(1)} %get-tuple-element.33.x_ref.refs_0_, ...), custom_call_target="tpu_custom_call", output_to_operand_aliasing={{0}: (0, {})} | custom-call | tf_op jit(solution)/shard_map/pallas_call | solution.py:263
  10.2 0.0 collective-permute-done.got_ref
  10.3 1.8 %collective-permute-start.2 = (bf16[2,128,256]{2,1,0:T(8,128)(2,1)S(1)}, bf16[2,128,256]{2,1,0:T(8,128)(2,1)S(1)}, u32[]{:S(2)}, u32[]{:S(2)}) collective-permute-start(bf16[2,128,256]{2,1,0:T(8,128)(2,1)S(1)} %get-tuple-element.41._), channel_id=1, source_target_pairs={{0,8},{4,12},{8,0},{12,4},{16,24},{20,28},{24,16},{28,20},{1,9},{5... | collective-permute-start | bytes 393224 | tf_op jit(solution)/shard_map/ppermute | solution.py:26
  12.1 1.2 %collective-permute-start.1 = (bf16[2,128,256]{2,1,0:T(8,128)(2,1)S(1)}, bf16[2,128,256]{2,1,0:T(8,128)(2,1)S(1)}, u32[]{:S(2)}, u32[]{:S(2)}) collective-permute-start(bf16[2,128,256]{2,1,0:T(8,128)(2,1)S(1)} %get-tuple-element.44), channel_id=1, source_target_pairs={{0,4},{4,0},{8,12},{12,8},{16,20},{20,16},{24,28},{28,24},{1,5},{5... | collective-permute-start | bytes 393224 | tf_op jit(solution)/shard_map/ppermute | solution.py:26
  13.3 1.4 %shard_map.59 = (s32[8,128]{1,0:T(8,128)S(4)}, bf16[2,128,256]{2,1,0:T(8,128)(2,1)S(1)}) custom-call(s32[8,128]{1,0:T(8,128)S(4)} %get-tuple-element.37.old_plan_ref, bf16[96,128,128]{2,1,0:T(8,128)(2,1)S(1)} %get-tuple-element.33.x_ref.refs_0_, bf16[2048,256]{1,0:T(8,128)(2,1)S(1)} %get-tuple-element.34.rhs_ref.refs_1_, ...), custom_call_target="tpu_custom_call", output_to_operand_aliasing={{0}: (0, {})} | custom-call | tf_op jit(solution)/shard_map/pallas_call | solution.py:263
  14.7 0.0 collective-permute-done.3.got_ref
  14.8 0.9 %collective-permute-start.5 = (bf16[2,128,256]{2,1,0:T(8,128)(2,1)S(1)}, bf16[2,128,256]{2,1,0:T(8,128)(2,1)S(1)}, u32[]{:S(2)}, u32[]{:S(2)}) collective-permute-start(bf16[2,128,256]{2,1,0:T(8,128)(2,1)S(1)} %get-tuple-element.51), channel_id=1, source_target_pairs={{0,4},{4,0},{8,12},{12,8},{16,20},{20,16},{24,28},{28,24},{1,5},{5... | collective-permute-start | bytes 393224 | tf_op jit(solution)/shard_map/ppermute | solution.py:26
  15.6 0.0 collective-permute-done.2.got_ref
  15.7 3.5 %collective-permute-start.4 = (bf16[2,128,256]{2,1,0:T(8,128)(2,1)S(1)}, bf16[2,128,256]{2,1,0:T(8,128)(2,1)S(1)}, u32[]{:S(2)}, u32[]{:S(2)}) collective-permute-start(bf16[2,128,256]{2,1,0:T(8,128)(2,1)S(1)} %get-tuple-element.48.refs_2_), channel_id=1, source_target_pairs={{0,24},{4,28},{8,16},{12,20},{16,8},{20,12},{24,0},{28,4},{1,25},{... | collective-permute-start | bytes 393224 | tf_op jit(solution)/shard_map/ppermute | solution.py:26
  19.2 0.0 collective-permute-done.1.refs_1_
  19.2 1.6 %shard_map.62 = (f32[17,128,256]{2,1,0:T(8,128)S(1)}, s32[8,128]{1,0:T(8,128)S(4)}) custom-call(s32[8,128]{1,0:T(8,128)S(4)} %get-tuple-element.42.old_plan_ref, bf16[96,128,128]{2,1,0:T(8,128)(2,1)S(1)} %get-tuple-element.33.x_ref.refs_0_, bf16[2,128,256]{2,1,0:T(8,128)(2,1)S(1)} %get-tuple-element.43.refs_2_.inner_ref, ...), custom_call_target="tpu_custom_call", output_to_operand_aliasing={{1}: (0, {})} | custom-call | tf_op jit(solution)/shard_map/pallas_call | solution.py:289
  20.8 0.0 collective-permute-done.5.got_ref
  20.8 0.5 %shard_map.63.old_ref = f32[17,128,256]{2,1,0:T(8,128)S(1)} custom-call(s32[8,128]{1,0:T(8,128)S(4)} %get-tuple-element.50.plan_ref, bf16[96,128,128]{2,1,0:T(8,128)(2,1)S(1)} %get-tuple-element.33.x_ref.refs_0_, f32[2,128,256]{2,1,0:T(8,128)S(1)} %get-tuple-element.47.refs_3_.refs_4_.own_ref, ...), custom_call_target="tpu_custom_call", output_to_operand_aliasing={{}: (4, {})} | custom-call | tf_op jit(solution)/shard_map/pallas_call | solution.py:301
  21.3 1.3 %collective-permute-done.4.got_ref = bf16[2,128,256]{2,1,0:T(8,128)(2,1)S(1)} collective-permute-done((bf16[2,128,256]{2,1,0:T(8,128)(2,1)S(1)}, bf16[2,128,256]{2,1,0:T(8,128)(2,1)S(1)}, u32[]{:S(2)}, u32[]{:S(2)}) %collective-permute-start.4) | collective-permute-done | bytes 131104 | tf_op jit(solution)/shard_map/ppermute | solution.py:26
  22.6 0.5 %shard_map.64 = (f32[17,128,256]{2,1,0:T(8,128)S(1)}, bf16[2,128,256]{2,1,0:T(8,128)(2,1)S(1)}, f32[1,4,128,256]{3,2,1,0:T(8,128)S(1)}, bf16[1,4,128,256]{3,2,1,0:T(8,128)(2,1)S(1)}) custom-call(s32[8,128]{1,0:T(8,128)S(4)} %get-tuple-element.50.plan_ref, bf16[96,128,128]{2,1,0:T(8,128)(2,1)S(1)} %get-tuple-element.33.x_ref.refs_0_, ...), custom_call_target="tpu_custom_call", output_to_operand_aliasing={{0}: (4, {})} | custom-call | tf_op jit(solution)/shard_map/pallas_call | solution.py:314
  23.2 0.1 collective-permute-start.7
  23.2 0.5 %shard_map.65 = (f32[17,128,256]{2,1,0:T(8,128)S(1)}, f32[1,4,128,256]{3,2,1,0:T(8,128)S(1)}, bf16[1,4,128,256]{3,2,1,0:T(8,128)(2,1)S(1)}) custom-call(s32[8,128]{1,0:T(8,128)S(4)} %get-tuple-element.50.plan_ref, bf16[96,128,128]{2,1,0:T(8,128)(2,1)S(1)} %get-tuple-element.33.x_ref.refs_0_, ...), custom_call_target="tpu_custom_call", output_to_operand_aliasing={{0}: (3, {})} | custom-call | tf_op jit(solution)/shard_map/pallas_call | solution.py:323
  23.8 0.5 %collective-permute-start.6 = (bf16[1,4,128,256]{3,2,1,0:T(8,128)(2,1)S(1)}, bf16[1,4,128,256]{3,2,1,0:T(8,128)(2,1)S(1)}, u32[]{:S(2)}, u32[]{:S(2)}) collective-permute-start(bf16[1,4,128,256]{3,2,1,0:T(8,128)(2,1)S(1)} %get-tuple-element.56), channel_id=1, source_target_pairs={{0,1},{1,0},{2,3},{3,2},{4,5},{5,4},{6,7},{7,6},{8,9},{9,8},{10,11... | collective-permute-start | bytes 786440 | tf_op jit(solution)/shard_map/ppermute | solution.py:26
  24.3 0.5 %collective-permute-done.7 = bf16[1,4,128,256]{3,2,1,0:T(8,128)(2,1)S(1)} collective-permute-done((bf16[1,4,128,256]{3,2,1,0:T(8,128)(2,1)S(1)}, bf16[1,4,128,256]{3,2,1,0:T(8,128)(2,1)S(1)}, u32[]{:S(2)}, u32[]{:S(2)}) %collective-permute-start.7) | collective-permute-done | bytes 262176 | tf_op jit(solution)/shard_map/ppermute | solution.py:26
  24.8 0.1 fusion.1
  24.8 1.4 %collective-permute-start.8 = (bf16[4,128,256]{2,1,0:T(8,128)(2,1)S(1)}, bf16[4,128,256]{2,1,0:T(8,128)(2,1)S(1)}, u32[]{:S(2)}, u32[]{:S(2)}) collective-permute-start(bf16[4,128,256]{2,1,0:T(8,128)(2,1)S(1)} %fusion.1), channel_id=1, source_target_pairs={{0,2},{1,3},{2,0},{3,1},{4,6},{5,7},{6,4},{7,5},{8,10},{9,11},{10,... | collective-permute-start | bytes 786440 | tf_op jit(solution)/shard_map/ppermute | solution.py:26
  26.3 0.0 collective-permute-done.6
  26.3 7.0 %collective-permute-done.8 = bf16[4,128,256]{2,1,0:T(8,128)(2,1)S(1)} collective-permute-done((bf16[4,128,256]{2,1,0:T(8,128)(2,1)S(1)}, bf16[4,128,256]{2,1,0:T(8,128)(2,1)S(1)}, u32[]{:S(2)}, u32[]{:S(2)}) %collective-permute-start.8) | collective-permute-done | bytes 262176 | tf_op jit(solution)/shard_map/ppermute | solution.py:26
  33.2 0.8 %fusion = bf16[4,128,256]{2,1,0:T(8,128)(2,1)} fusion(bf16[4,128,256]{2,1,0:T(8,128)(2,1)S(1)} %collective-permute-done.8, f32[1,4,128,256]{3,2,1,0:T(8,128)S(1)} %get-tuple-element.55, bf16[1,4,128,256]{3,2,1,0:T(8,128)(2,1)S(1)} %collective-permute-done.6), kind=kLoop, calls=%fused_computation.1 | loop fusion | flops 655360 | bytes 1310720 | tf_op jit(solution)/shard_map/convert_element_type | solution.py:345
  (3 shorter events, 0.1 us)
Async XLA Ops:
  3.4 6.9 %collective-permute-start = (bf16[2,128,256]{2,1,0:T(8,128)(2,1)S(1)}, bf16[2,128,256]{2,1,0:T(8,128)(2,1)S(1)}, u32[]{:S(2)}, u32[]{:S(2)}) collective-permute-start(bf16[2,128,256]{2,1,0:T(8,128)(2,1)S(1)} %get-tuple-element.38), channel_id=1, source_target_pairs={{0,4},{4,0},{8,12},{12,8},{16,20},{20,16},{24,28},{28,24},{1,5},{5... | collective-permute-start | bytes 393224 | tf_op jit(solution)/shard_map/ppermute | solution.py:26
  6.9 7.8 %collective-permute-start.3 = (bf16[2,128,256]{2,1,0:T(8,128)(2,1)S(1)}, bf16[2,128,256]{2,1,0:T(8,128)(2,1)S(1)}, u32[]{:S(2)}, u32[]{:S(2)}) collective-permute-start(bf16[2,128,256]{2,1,0:T(8,128)(2,1)S(1)} %get-tuple-element.46), channel_id=1, source_target_pairs={{0,8},{4,12},{8,0},{12,4},{16,24},{20,28},{24,16},{28,20},{1,9},{5... | collective-permute-start | bytes 393224 | tf_op jit(solution)/shard_map/ppermute | solution.py:26
  10.3 5.3 %collective-permute-start.2 = (bf16[2,128,256]{2,1,0:T(8,128)(2,1)S(1)}, bf16[2,128,256]{2,1,0:T(8,128)(2,1)S(1)}, u32[]{:S(2)}, u32[]{:S(2)}) collective-permute-start(bf16[2,128,256]{2,1,0:T(8,128)(2,1)S(1)} %get-tuple-element.41._), channel_id=1, source_target_pairs={{0,8},{4,12},{8,0},{12,4},{16,24},{20,28},{24,16},{28,20},{1,9},{5... | collective-permute-start | bytes 393224 | tf_op jit(solution)/shard_map/ppermute | solution.py:26
  12.1 7.1 %collective-permute-start.1 = (bf16[2,128,256]{2,1,0:T(8,128)(2,1)S(1)}, bf16[2,128,256]{2,1,0:T(8,128)(2,1)S(1)}, u32[]{:S(2)}, u32[]{:S(2)}) collective-permute-start(bf16[2,128,256]{2,1,0:T(8,128)(2,1)S(1)} %get-tuple-element.44), channel_id=1, source_target_pairs={{0,4},{4,0},{8,12},{12,8},{16,20},{20,16},{24,28},{28,24},{1,5},{5... | collective-permute-start | bytes 393224 | tf_op jit(solution)/shard_map/ppermute | solution.py:26
  14.8 6.0 %collective-permute-start.5 = (bf16[2,128,256]{2,1,0:T(8,128)(2,1)S(1)}, bf16[2,128,256]{2,1,0:T(8,128)(2,1)S(1)}, u32[]{:S(2)}, u32[]{:S(2)}) collective-permute-start(bf16[2,128,256]{2,1,0:T(8,128)(2,1)S(1)} %get-tuple-element.51), channel_id=1, source_target_pairs={{0,4},{4,0},{8,12},{12,8},{16,20},{20,16},{24,28},{28,24},{1,5},{5... | collective-permute-start | bytes 393224 | tf_op jit(solution)/shard_map/ppermute | solution.py:26
  15.7 6.9 %collective-permute-start.4 = (bf16[2,128,256]{2,1,0:T(8,128)(2,1)S(1)}, bf16[2,128,256]{2,1,0:T(8,128)(2,1)S(1)}, u32[]{:S(2)}, u32[]{:S(2)}) collective-permute-start(bf16[2,128,256]{2,1,0:T(8,128)(2,1)S(1)} %get-tuple-element.48.refs_2_), channel_id=1, source_target_pairs={{0,24},{4,28},{8,16},{12,20},{16,8},{20,12},{24,0},{28,4},{1,25},{... | collective-permute-start | bytes 393224 | tf_op jit(solution)/shard_map/ppermute | solution.py:26
  23.2 1.6 %collective-permute-start.7 = (bf16[1,4,128,256]{3,2,1,0:T(8,128)(2,1)S(1)}, bf16[1,4,128,256]{3,2,1,0:T(8,128)(2,1)S(1)}, u32[]{:S(2)}, u32[]{:S(2)}) collective-permute-start(bf16[1,4,128,256]{3,2,1,0:T(8,128)(2,1)S(1)} %get-tuple-element.58), channel_id=1, source_target_pairs={{0,1},{1,0},{2,3},{3,2},{4,5},{5,4},{6,7},{7,6},{8,9},{9,8},{10,11... | collective-permute-start | bytes 786440 | tf_op jit(solution)/shard_map/ppermute | solution.py:26
  23.8 2.5 %collective-permute-start.6 = (bf16[1,4,128,256]{3,2,1,0:T(8,128)(2,1)S(1)}, bf16[1,4,128,256]{3,2,1,0:T(8,128)(2,1)S(1)}, u32[]{:S(2)}, u32[]{:S(2)}) collective-permute-start(bf16[1,4,128,256]{3,2,1,0:T(8,128)(2,1)S(1)} %get-tuple-element.56), channel_id=1, source_target_pairs={{0,1},{1,0},{2,3},{3,2},{4,5},{5,4},{6,7},{7,6},{8,9},{9,8},{10,11... | collective-permute-start | bytes 786440 | tf_op jit(solution)/shard_map/ppermute | solution.py:26
  24.8 8.4 %collective-permute-start.8 = (bf16[4,128,256]{2,1,0:T(8,128)(2,1)S(1)}, bf16[4,128,256]{2,1,0:T(8,128)(2,1)S(1)}, u32[]{:S(2)}, u32[]{:S(2)}) collective-permute-start(bf16[4,128,256]{2,1,0:T(8,128)(2,1)S(1)} %fusion.1), channel_id=1, source_target_pairs={{0,2},{1,3},{2,0},{3,1},{4,6},{5,7},{6,4},{7,5},{8,10},{9,11},{10,... | collective-permute-start | bytes 786440 | tf_op jit(solution)/shard_map/ppermute | solution.py:26
